TPU v7x, 128 devices: a whole 4x4x4 slice. The times are simulated.
128 devices in a mesh: section: 8 (over x, y_lo), attn: 16 (over y_hi, z, core).
Axes of the slice: x: 4, y: 4 (y_hi: 2, y_lo: 2; y = y_hi * 2 + y_lo), z: 4, core: 2. Of those that a mesh axis runs over, the one named last changes fastest.
Arguments:
- c_query: bfloat16 [64, 1536], P('section'), may hold values from -6 to 6
- up_query: bfloat16 [1536, 16384], P('section', 'attn'), may hold values from -0.15625 to 0.15625
- rope_query: bfloat16 [1536, 8192], P('section', 'attn'), may hold values from -0.15625 to 0.15625
- key_up: bfloat16 [512, 16384], P('section', 'attn'), may hold values from -0.5 to 0.5
- value_up: bfloat16 [512, 16384], P('section', 'attn'), may hold values from -0.5 to 0.5
- out_weight: bfloat16 [16384, 7168], P(None, ('section', 'attn')), may hold values from -0.09375 to 0.09375
- cache: bfloat16 [64, 8192, 576], P('section', 'attn'), may hold values from -340 to 340
- new_entry: bfloat16 [64, 576], P('section'), may hold values from -6 to 6
- lengths: int32 [64], P('section'), may hold values from 1024 to 8192, as said below
Outputs:
- mixed: bfloat16 [64, 7168], P('section', 'attn')
Inputs may be any that keep to these rules, and one draw needn't show every extreme that they name: `lengths`: each row's count of filled slots; some row has all 8192 filled.
All inputs are finite; a program needn't handle non-finite values.
Results may differ from a plain program's by a relative error of at most 0.012.
The roundings to bfloat16 on the way count: a program that leaves them out, or rounds other values in their place, can miss the bound.
Values may be sent and summed in bfloat16 or wider, within the bound.
No kernel may reach another device: no remote copies, remote signals or barrier semaphores. Data moves between devices by JAX's collectives and lax.ppermute only.
A program may use at most 256 MiB of HBM per device.

v0:
```python
import jax
import jax.numpy as jnp
from jax import lax
from jax.sharding import PartitionSpec as P

D = 7168
QL = 1536
KL = 512
NOPE = 128
ROPE = 64


def rotate_pairs(rope_part, position):
    half_width = rope_part.shape[-1] // 2
    freq_rates = 10000.0 ** (-jnp.arange(half_width, dtype=jnp.float32) / half_width)
    angles = position[..., None] * freq_rates
    cosine = jnp.cos(angles)
    sine_part = jnp.sin(angles)
    lower_half = rope_part[..., :half_width]
    upper_half = rope_part[..., half_width:]
    return jnp.concatenate(
        [
            lower_half * cosine - upper_half * sine_part,
            lower_half * sine_part + upper_half * cosine,
        ],
        axis=-1,
    )


def on_device(
    c_query, up_query, rope_query, key_up, value_up, out_weight, cache, new_entry, lengths
):
    row_count = c_query.shape[0]
    heads_dev = key_up.shape[1] // NOPE
    score_scale = (NOPE + ROPE) ** (-0.5)
    position = lengths.astype(jnp.float32)[:, None]
    full_query, full_rope, full_key, full_value = (
        lax.all_gather(up_query, "section", axis=0, tiled=True),
        lax.all_gather(rope_query, "section", axis=0, tiled=True),
        lax.all_gather(key_up, "section", axis=0, tiled=True),
        lax.all_gather(value_up, "section", axis=0, tiled=True),
    )
    absorbed = jnp.einsum(
        "qhd,khd->hqk",
        full_query.reshape(QL, heads_dev, NOPE),
        full_key.reshape(KL, heads_dev, NOPE),
        preferred_element_type=jnp.float32,
    ).astype(jnp.bfloat16)
    latent_query = jnp.einsum("rq,hqk->rhk", c_query, absorbed, preferred_element_type=jnp.float32)
    rope_rows = jnp.dot(c_query, full_rope, preferred_element_type=jnp.float32).reshape(
        row_count, heads_dev, ROPE
    )
    queries_own = jnp.concatenate(
        [latent_query, rotate_pairs(rope_rows, position)], axis=-1
    ).astype(jnp.bfloat16)
    own_score = (
        jnp.einsum("rhc,rc->rh", queries_own, new_entry, preferred_element_type=jnp.float32)
        * score_scale
    )
    all_query = lax.all_gather(queries_own, "attn", axis=1, tiled=True)
    span = cache.shape[1]
    first_slot = lax.axis_index("attn") * span
    valid_mask = (first_slot + jnp.arange(span, dtype=jnp.int32))[None, :] < lengths[:, None]
    scores = (
        jnp.einsum("rhc,rlc->rhl", all_query, cache, preferred_element_type=jnp.float32)
        * score_scale
    )
    masked = jnp.where(valid_mask[:, None, :], scores, -1e30)
    top_score = jnp.max(masked, axis=-1)
    probability = jnp.where(valid_mask[:, None, :], jnp.exp(masked - top_score[..., None]), 0.0)
    mass_sum = jnp.sum(probability, axis=-1)
    weighted = jnp.einsum(
        "rhl,rlc->rhc",
        probability.astype(jnp.bfloat16),
        cache[:, :, :KL],
        preferred_element_type=jnp.float32,
    )
    partial_value = weighted / jnp.maximum(mass_sum, 1.0)[..., None]
    part_out, part_top, part_mass = (
        lax.all_to_all(partial_value[None], "attn", split_axis=2, concat_axis=0, tiled=True),
        lax.all_to_all(top_score[None], "attn", split_axis=2, concat_axis=0, tiled=True),
        lax.all_to_all(mass_sum[None], "attn", split_axis=2, concat_axis=0, tiled=True),
    )
    highest = jnp.maximum(jnp.max(part_top, axis=0), own_score)
    block_weight = part_mass * jnp.exp(part_top - highest[None])
    new_weight = jnp.exp(own_score - highest)
    numer = jnp.sum(block_weight[..., None] * part_out, axis=0) + new_weight[..., None] * new_entry[
        :, None, :KL
    ].astype(jnp.float32)
    denom = jnp.sum(block_weight, axis=0) + new_weight
    latent_out = (numer / denom[..., None]).astype(jnp.bfloat16)
    value_heads = full_value.reshape(KL, heads_dev, NOPE)
    swapped = lax.all_to_all(out_weight, "attn", split_axis=0, concat_axis=1, tiled=True)
    owned_rows = lax.all_gather(swapped, "section", axis=1, tiled=True)
    absorbed_out = jnp.einsum(
        "khd,hdn->hkn",
        value_heads,
        owned_rows.reshape(heads_dev, NOPE, D),
        preferred_element_type=jnp.float32,
    ).astype(jnp.bfloat16)
    mixed_part = jnp.dot(
        latent_out.reshape(row_count, heads_dev * KL),
        absorbed_out.reshape(heads_dev * KL, D),
        preferred_element_type=jnp.float32,
    )
    return lax.psum_scatter(mixed_part, "attn", scatter_dimension=1, tiled=True).astype(
        jnp.bfloat16
    )


def solution(mesh):
    return jax.shard_map(
        on_device,
        mesh=mesh,
        in_specs=(
            P("section", None),
            P("section", "attn"),
            P("section", "attn"),
            P("section", "attn"),
            P("section", "attn"),
            P(None, ("section", "attn")),
            P("section", "attn", None),
            P("section", None),
            P("section"),
        ),
        out_specs=P("section", "attn"),
        check_vma=False,
    )
```

profile of v0, /device:TPU:7, one launch (start us, length us, event | category | flops | bytes accessed | tf_op | source)
XLA Modules:
  0.0 705.0 jit_solution(8565028098090993974)
XLA Ops:
  6.5 0.0 copy-start
  6.5 0.0 all-gather.9.cloned.1.call-start
  6.5 0.7 all-gather.9.cloned.1.call-update
  7.3 0.0 all-gather.11.cloned.1.call-start
  7.3 0.7 all-gather.11.cloned.1.call-update
  8.0 0.0 all-gather.7.cloned.1.call-start
  8.1 0.7 all-gather.7.cloned.1.call-update
  8.7 0.0 all-gather.13.cloned.1.call-start
  8.8 0.7 convert_element_type.24
  9.5 0.1 multiply_cosine_fusion
  9.6 34.7 %all-gather.9.cloned.1.call-done = bf16[512,1024]{1,0:T(8,128)(2,1)} async-done(((bf16[64,1024]{1,0:T(8,128)(2,1)}), bf16[512,1024]{1,0:T(8,128)(2,1)}) %all-gather.9.cloned.1.call-update) | async-done | bytes 1048592 | tf_op jit(solution)/shard_map/all_gather | solution.py:40
  44.2 2.3 copy.61
  46.5 45.2 %all-gather.11.cloned.1.call-done = bf16[1536,512]{1,0:T(8,128)(2,1)} async-done(((bf16[192,512]{1,0:T(8,128)(2,1)}), bf16[1536,512]{1,0:T(8,128)(2,1)}) %all-gather.11.cloned.1.call-update) | async-done | bytes 1572880 | tf_op jit(solution)/shard_map/all_gather | solution.py:39
  91.7 0.0 copy-done
  91.7 1.7 fusion.42
  93.4 0.1 reshape.129
  93.5 0.1 fusion.41
  93.6 72.7 %all-gather.7.cloned.1.call-done = bf16[1536,1024]{1,0:T(8,128)(2,1)} async-done(((bf16[192,1024]{1,0:T(8,128)(2,1)}), bf16[1536,1024]{1,0:T(8,128)(2,1)}) %all-gather.7.cloned.1.call-update) | async-done | bytes 3145744 | tf_op jit(solution)/shard_map/all_gather | solution.py:38
  166.3 3.2 copy.60
  169.5 6.9 fusion.17
  176.4 0.7 pad_maximum_fusion
  177.1 0.0 all-gather.13.cloned.1.call-update
  177.1 0.0 all-gather.15.cloned.1.call-start
  177.2 0.5 all-gather.15.cloned.1.call-update
  177.7 0.0 all-gather.17.cloned.1.call-start
  177.8 1.6 copy.109
  179.4 0.0 copy-start.4
  179.4 34.0 %all_to_all.73 = bf16[16,1024,56]{1,2,0:T(8,128)(2,1)} all-to-all(bf16[16,1024,56]{1,2,0:T(8,128)(2,1)S(1)} %bitcast.63), channel_id=1, replica_groups=mesh['section'=8,'attn'=16] {'attn'}, dimensions={0} | all-to-all | bytes 3670016 | tf_op jit(solution)/shard_map/all_to_all | solution.py:93
  213.5 0.0 all-gather.17.cloned.1.call-update
  213.5 0.0 copy-done.4
  213.5 0.1 broadcast_compare_fusion
  213.6 15.4 %all-gather.13.cloned.1.call-done = bf16[8,128,576]{2,0,1:T(8,128)(2,1)} async-done(((bf16[8,8,576]{2,0,1:T(8,128)(2,1)}), bf16[8,128,576]{2,0,1:T(8,128)(2,1)}) %all-gather.13.cloned.1.call-update) | async-done | bytes 1179664 | tf_op jit(solution)/shard_map/all_gather | solution.py:60
  229.0 3.9 fusion.11
  232.9 0.7 fusion.13
  233.6 0.7 copy.67
  234.3 4.0 all-to-all-start
  238.3 0.7 copy.69
  239.1 7.0 all-to-all-done
  246.1 4.1 all-to-all-start.1
  250.2 3.4 divide_bitcast_fusion
  253.6 2.5 copy.72
  256.1 0.0 copy-start.3
  256.1 2.3 all-to-all-done.1
  258.4 5.2 all-to-all-start.2
  263.5 0.0 copy-start.2
  263.5 0.2 reduce-scatter.4.cloned.1.call-start
  263.8 0.0 copy-done.3
  263.8 0.0 all-gather.15.cloned.1.call-done
  263.8 1.5 copy.74
  265.3 0.0 copy-done.2
  265.3 0.1 fusion.28
  265.5 0.1 copy.85
  265.6 0.1 copy.86
  265.8 59.6 %all-to-all-done.2 = f32[1,8,128,512]{3,1,0,2:T(8,128)S(1)} async-done(((f32[1,8,128,512]{3,1,0,2:T(8,128)}), f32[1,8,128,512]{3,1,0,2:T(8,128)S(1)}, u32[]{:S(2)}, u32[]{:S(2)}) %all-to-all-start.2) | async-done | bytes 2097184 | tf_op jit(solution)/shard_map/all_to_all | solution.py:80
  325.4 1.1 fusion.10
  326.5 0.1 divide_convert_fusion
  326.6 238.1 %all-gather.17.cloned.1.call-done = bf16[1024,7168]{0,1:T(8,128)(2,1)} async-done(((bf16[1024,896]{0,1:T(8,128)(2,1)}), bf16[1024,7168]{0,1:T(8,128)(2,1)}) %all-gather.17.cloned.1.call-update) | async-done | bytes 14680080 | tf_op jit(solution)/shard_map/all_gather | solution.py:94
  564.7 18.4 %copy.76 = bf16[1024,7168]{1,0:T(8,128)(2,1)} copy(bf16[1024,7168]{0,1:T(8,128)(2,1)} %all-gather.17.cloned.1.call-done) | data formatting | bytes 29360128 | tf_op jit(solution)/shard_map/all_gather | solution.py:94
  583.1 0.0 copy-start.1
  583.1 34.3 %fusion.4 = f32[7168,8]{1,0:T(8,128)} fusion(bf16[512,8,128]{0,2,1:T(8,128)(2,1)S(1)} %bitcast.66, bf16[8,128,7168]{2,1,0:T(8,128)(2,1)} %bitcast.60, bf16[8,8,512]{2,1,0:T(8,128)(2,1)S(1)} %divide_convert_fusion), kind=kOutput, calls=%fused_computation.4 | convolution fusion | flops 8015314944 | bytes 16023552 | tf_op jit(solution)/shard_map/dot_general | solution.py:101
  617.4 0.0 reduce-scatter.4.cloned.1.call-update
  617.4 79.1 %reduce-scatter.4.cloned.1.call-done = f32[448,8]{1,0:T(8,128)} async-done(((f32[7168,8]{1,0:T(8,128)}), f32[448,8]{1,0:T(8,128)}) %reduce-scatter.4.cloned.1.call-update) | async-done | bytes 14352
  696.5 1.6 copy.88
  698.2 0.0 copy-done.1
  (9 shorter events, 0.1 us)
Async XLA Ops:
  6.5 85.2 %copy-start = (bf16[8,1536]{1,0:T(8,128)(2,1)S(1)}, bf16[8,1536]{1,0:T(8,128)(2,1)}, u32[]{:S(2)}) copy-start(bf16[8,1536]{1,0:T(8,128)(2,1)} %param.9) | copy-start | bytes 73732
  6.5 37.7 %all-gather.9.cloned.1.call-start = ((), (), s32[]{:S(2)}) async-start(), calls=%async_computation.6 | async-start | bytes 1179648 | tf_op jit(solution)/shard_map/all_gather | solution.py:40
  7.3 84.5 %all-gather.11.cloned.1.call-start = ((), (), s32[]{:S(2)}) async-start(), calls=%async_computation.7 | async-start | bytes 1769472 | tf_op jit(solution)/shard_map/all_gather | solution.py:39
  8.0 158.3 %all-gather.7.cloned.1.call-start = ((), (), s32[]{:S(2)}) async-start(), calls=%async_computation.5 | async-start | bytes 3538944 | tf_op jit(solution)/shard_map/all_gather | solution.py:38
  8.7 220.2 %all-gather.13.cloned.1.call-start = ((), (), s32[]{:S(2)}) async-start(), calls=%async_computation.8 | async-start | bytes 1392640 | tf_op jit(solution)/shard_map/all_gather | solution.py:60
  177.1 86.7 %all-gather.15.cloned.1.call-start = ((), (), s32[]{:S(2)}) async-start(), calls=%async_computation.9 | async-start | bytes 1179648 | tf_op jit(solution)/shard_map/all_gather | solution.py:41
  177.7 387.0 %all-gather.17.cloned.1.call-start = ((), (), s32[]{:S(2)}) async-start(), calls=%async_computation.10 | async-start | bytes 16515072 | tf_op jit(solution)/shard_map/all_gather | solution.py:94
  179.4 34.1 %copy-start.4 = (s32[8]{0:T(128)S(1)}, s32[8]{0:T(128)}, u32[]{:S(2)}) copy-start(s32[8]{0:T(128)} %param.17) | copy-start | bytes 100
  234.3 11.8 %all-to-all-start = ((f32[1,8,128]{1,0,2:T(1,128)}), f32[1,8,128]{1,0,2:T(1,128)S(1)}, u32[]{:S(2)}, u32[]{:S(2)}) async-start(f32[1,8,128]{1,0,2:T(1,128)} %copy.67), calls=%async_computation | async-start | bytes 131072 | tf_op jit(solution)/shard_map/all_to_all | solution.py:82
  246.1 12.3 %all-to-all-start.1 = ((f32[1,8,128]{1,0,2:T(1,128)}), f32[1,8,128]{1,0,2:T(1,128)S(1)}, u32[]{:S(2)}, u32[]{:S(2)}) async-start(f32[1,8,128]{1,0,2:T(1,128)} %copy.69), calls=%async_computation.1 | async-start | bytes 131072 | tf_op jit(solution)/shard_map/all_to_all | solution.py:81
  256.1 7.7 %copy-start.3 = (bf16[8,576]{1,0:T(8,128)(2,1)S(1)}, bf16[8,576]{1,0:T(8,128)(2,1)}, u32[]{:S(2)}) copy-start(bf16[8,576]{1,0:T(8,128)(2,1)} %param.16) | copy-start | bytes 27652
  258.4 67.0 %all-to-all-start.2 = ((f32[1,8,128,512]{3,1,0,2:T(8,128)}), f32[1,8,128,512]{3,1,0,2:T(8,128)S(1)}, u32[]{:S(2)}, u32[]{:S(2)}) async-start(f32[1,8,128,512]{3,1,0,2:T(8,128)} %copy.72), calls=%async_computation.2 | async-start | bytes 4194304 | tf_op jit(solution)/shard_map/all_to_all | solution.py:80
  263.5 1.8 copy-start.2
  263.5 433.0 %reduce-scatter.4.cloned.1.call-start = ((), (), s32[]{:S(2)}) async-start(), calls=%async_computation.11 | async-start | bytes 3899392
  583.1 115.1 %copy-start.1 = (bf16[8,1536]{1,0:T(8,128)(2,1)S(1)}, bf16[8,1536]{1,0:T(8,128)(2,1)}, u32[]{:S(2)}) copy-start(bf16[8,1536]{1,0:T(8,128)(2,1)} %param.9) | copy-start | bytes 73732
Sparse Core Ops, SparseCore 0:
  9.0 35.1 all-gather.8
  45.9 45.7 all-gather.10
  93.4 72.9 all-gather.6
  177.3 51.6 all-gather.12
  230.4 32.3 all-gather.14
  264.3 300.3 all-gather.16
  617.6 78.9 reduce-scatter.3
where the time goes:
time: 708 us; the launch traced here: 705 us
  waiting for transfers between devices  557 us (79%)
  matrix products  50.4 us (7%)
  blocking collectives  34 us (5%)
  local copies, waits for them, and re-layouts  32.9 us (5%)
  starting transfers between devices  13.7 us (2%)
  between operations  13.7 us (2%)
    all_gather x1, waiting for transfers between devices, on_device(): owned_rows = lax.all_gather(swapped, 'section', axis=1, tiled=True)  238 us
    unnamed x8, waiting for transfers between devices  81.8 us
    all_gather x1, waiting for transfers between devices, on_device(): lax.all_gather(up_query, 'section', axis=0, tiled=True)  72.7 us
    all_to_all x1, waiting for transfers between devices, on_device(): lax.all_to_all(partial_value[None], 'attn', split_axis=2, concat_axis=0,...  59.6 us
    all_gather x1, waiting for transfers between devices, on_device(): lax.all_gather(rope_query, 'section', axis=0, tiled=True)  45.2 us
    all_gather x1, waiting for transfers between devices, on_device(): lax.all_gather(key_up, 'section', axis=0, tiled=True)  34.7 us
    dot_general x1, matrix products, on_device(): jnp.dot(latent_out.reshape(row_count, heads_dev * KL), absorbed_out.resha...  34.3 us
    all_to_all x1, blocking collectives, on_device(): lax.all_to_all(out_weight, 'attn', split_axis=0, concat_axis=1, tiled=True)  34 us
  transfers between devices with their start and end apart: 10, of which 9 were waited for; matrix products, arithmetic and copies ran while one was open for 3% of the time, Pallas kernels for 0%

commit v1 on v0

v1 whole, which is shorter than its diff:
```python
import functools

import jax
import jax.numpy as jnp
from jax import lax
from jax.experimental import pallas as pl
from jax.experimental.pallas import tpu as pltpu
from jax.sharding import Mesh
from jax.sharding import PartitionSpec as P

KL = 512
NOPE = 128
ROPE = 64
QDIM = KL + ROPE
HDEV = 8
RDEV = 8
PACK = KL + 128
SCALE = (NOPE + ROPE) ** -0.5
NEG = -1e30

ATTN = ("yh", "z", "core")
ALL = ("section",) + ATTN
bf16 = jnp.bfloat16
f32 = jnp.float32


def swap(x, axis, mask):
    names, size = (("section",), 8) if axis == "section" else (ATTN, 16)
    return lax.ppermute(x, names, [(i, i ^ mask) for i in range(size)])


def exchange(x, names):
    return lax.all_to_all(x, names, 0, 0, tiled=True)


def split3(x):
    a = x.astype(bf16).astype(f32)
    b = (x - a).astype(bf16).astype(f32)
    return a, b, x - a - b


def pack_stats(top, mass):
    terms = split3(top) + split3(mass)
    lane = lax.broadcasted_iota(jnp.int32, (top.shape[0], 128), 1)
    out = jnp.zeros((top.shape[0], 128), f32)
    for i, term in enumerate(terms):
        out = jnp.where(lane == i, term, out)
    return out


def unpack_stats(packed):
    top = packed[:, 0:1] + packed[:, 1:2] + packed[:, 2:3]
    mass = packed[:, 3:4] + packed[:, 4:5] + packed[:, 5:6]
    return top, mass


def query_kernel(order_ref, part_ref, key_ref, cos_ref, sin_ref, out_ref, key_scr, out_scr):
    q = part_ref[0]
    for i in range(1, 8):
        q = q + part_ref[i]
    for t in range(8):
        key_scr[t * 64:(t + 1) * 64, :] = key_ref[order_ref[t]]
    rope = q[:, HDEV * NOPE:]
    lane = lax.broadcasted_iota(jnp.int32, rope.shape, 1)
    up = pltpu.roll(rope, rope.shape[1] - ROPE // 2, 1)
    down = pltpu.roll(rope, ROPE // 2, 1)
    other = jnp.where(lane % ROPE < ROPE // 2, up, down)
    rope = rope * cos_ref[...] + other * sin_ref[...]
    for h in range(HDEV):
        qh = q[:, h * NOPE:(h + 1) * NOPE]
        hi = qh.astype(bf16)
        lo = (qh - hi.astype(f32)).astype(bf16)
        lhs = jnp.concatenate([hi.astype(f32), lo.astype(f32)], axis=0).astype(bf16)
        lat = lax.dot_general(
            lhs,
            key_scr[:, h * NOPE:(h + 1) * NOPE],
            (((1,), (1,)), ((), ())),
            preferred_element_type=f32,
        )
        lat = lat[0:8] + lat[8:16]
        tail = rope[:, h * ROPE:(h + 1) * ROPE]
        tail = jnp.concatenate([tail, jnp.zeros_like(tail)], axis=1)
        for j in range(4):
            out_scr[j, pl.ds(h, RDEV, stride=HDEV), :] = lat[:, j * 128:(j + 1) * 128]
        out_scr[4, pl.ds(h, RDEV, stride=HDEV), :] = tail
    for j in range(4):
        out_ref[:, j * 128:(j + 1) * 128] = out_scr[j].astype(bf16)
    out_ref[:, KL:QDIM] = out_scr[4, :, 0:ROPE].astype(bf16)


def make_queries(order, parts, key_blocks, cos, sin):
    vmem = pl.BlockSpec(memory_space=pltpu.VMEM)
    return pl.pallas_call(
        query_kernel,
        out_shape=jax.ShapeDtypeStruct((RDEV * HDEV, QDIM), bf16),
        in_specs=[pl.BlockSpec(memory_space=pltpu.SMEM)] + [vmem] * 4,
        out_specs=vmem,
        scratch_shapes=[
            pltpu.VMEM((KL, HDEV * NOPE), bf16),
            pltpu.VMEM((5, RDEV * HDEV, 128), f32),
        ],
        compiler_params=pltpu.CompilerParams(vmem_limit_bytes=24 * 1024 * 1024),
        name="make_queries",
    )(order, parts, key_blocks, cos, sin)


def attend_kernel(
    len_ref, at_ref, qa_ref, qb_ref, cache_ref, new_ref, keep_ref, send_ref, q_scr
):
    step = pl.program_id(0)

    @pl.when(step == 0)
    def _():
        q_scr[0:8] = qa_ref[...].astype(f32)
        q_scr[8:16] = qb_ref[...].astype(f32)

    first, owner = at_ref[0], at_ref[1]
    sends = []
    for i in range(2):
        row = step * 2 + i
        length = len_ref[row]
        at = pl.multiple_of(row * 8, 8)
        q = q_scr[:, pl.ds(at, 8), :].reshape(128, QDIM)
        keys = cache_ref[i]
        new = new_ref[i].astype(f32)
        own = jnp.sum(q * new, axis=1, keepdims=True) * SCALE
        score = (
            lax.dot_general(
                q.astype(bf16), keys, (((1,), (1,)), ((), ())), preferred_element_type=f32
            )
            * SCALE
        )
        slot = lax.broadcasted_iota(jnp.int32, score.shape, 1) + first
        valid = slot < length
        score = jnp.where(valid, score, NEG)
        top = jnp.max(score, axis=1, keepdims=True)
        prob = jnp.where(valid, jnp.exp(score - top), 0.0)
        mass = jnp.sum(prob, axis=1, keepdims=True)
        num = jnp.dot(prob.astype(bf16), keys[:, :KL], preferred_element_type=f32)
        mine = owner == 1
        own = jnp.where(mine, own, NEG)
        best = jnp.maximum(top, own)
        scale_old = jnp.exp(top - best)
        scale_new = jnp.where(mine, jnp.exp(own - best), 0.0)
        num = num * scale_old + scale_new * new[:, :KL]
        mass = mass * scale_old + scale_new
        stats = pack_stats(best, mass)
        keep_ref[:, pl.ds(at, 8), 0:KL] = num[0:64].reshape(8, 8, KL)
        keep_ref[:, pl.ds(at, 8), KL:PACK] = stats[0:64].reshape(8, 8, 128)
        sends.append(
            jnp.concatenate([num[64:128], stats[64:128]], axis=1).reshape(8, 8, PACK)
        )
    at = pl.multiple_of(step * 16, 16)
    send_ref[:, pl.ds(at, 16), :] = jnp.concatenate(sends, axis=1).astype(bf16)


def attend(lengths, place, qa, qb, cache, new):
    full = lambda *shape: pl.BlockSpec(shape, lambda r, *_: (0,) * len(shape))
    grid_spec = pltpu.PrefetchScalarGridSpec(
        num_scalar_prefetch=2,
        grid=(RDEV // 2,),
        in_specs=[
            full(8, 64, QDIM),
            full(8, 64, QDIM),
            pl.BlockSpec((2, cache.shape[1], QDIM), lambda r, *_: (r, 0, 0)),
            pl.BlockSpec((2, 1, QDIM), lambda r, *_: (r, 0, 0)),
        ],
        out_specs=[full(8, 64, PACK), full(8, 64, PACK)],
        scratch_shapes=[pltpu.VMEM((16, 64, QDIM), f32)],
    )
    return pl.pallas_call(
        attend_kernel,
        grid_spec=grid_spec,
        out_shape=[
            jax.ShapeDtypeStruct((8, 64, PACK), f32),
            jax.ShapeDtypeStruct((8, 64, PACK), bf16),
        ],
        compiler_params=pltpu.CompilerParams(vmem_limit_bytes=40 * 1024 * 1024),
        name="attend",
    )(lengths, place, qa, qb, cache, new)


def merge_kernel(keep_ref, got_ref, out_ref):
    for i in range(8):
        mine = keep_ref[i]
        other = got_ref[i].astype(f32)
        top_a, mass_a = unpack_stats(mine[:, KL:])
        top_b, mass_b = unpack_stats(other[:, KL:])
        best = jnp.maximum(top_a, top_b)
        wa, wb = jnp.exp(top_a - best), jnp.exp(top_b - best)
        num = mine[:, :KL] * wa + other[:, :KL] * wb
        out_ref[i, :, 0:KL] = num.astype(bf16)
        out_ref[i, :, KL:PACK] = pack_stats(best, mass_a * wa + mass_b * wb).astype(bf16)


def merge(keep, got):
    vmem = pl.BlockSpec(memory_space=pltpu.VMEM)
    return pl.pallas_call(
        merge_kernel,
        out_shape=jax.ShapeDtypeStruct((8, 64, PACK), bf16),
        in_specs=[vmem, vmem],
        out_specs=vmem,
        compiler_params=pltpu.CompilerParams(vmem_limit_bytes=24 * 1024 * 1024),
        name="merge",
    )(keep, got)


def combine_kernel(got_ref, value_ref, out_ref, lat_scr):
    tops, masses = [], []
    for i in range(8):
        top, mass = unpack_stats(got_ref[i, :, KL:PACK].astype(f32))
        tops.append(top)
        masses.append(mass)
    best = functools.reduce(jnp.maximum, tops)
    num = jnp.zeros((64, KL), f32)
    den = jnp.zeros((64, 1), f32)
    for i in range(8):
        w = jnp.exp(tops[i] - best)
        num = num + got_ref[i, :, 0:KL].astype(f32) * w
        den = den + masses[i] * w
    lat = num / den
    for j in range(4):
        lat_scr[j] = lat[:, j * 128:(j + 1) * 128]
    for h in range(HDEV):
        lat = jnp.concatenate(
            [lat_scr[j, pl.ds(h, RDEV, stride=HDEV), :] for j in range(4)], axis=1
        ).astype(bf16)
        out_ref[:, h * NOPE:(h + 1) * NOPE] = jnp.dot(
            lat, value_ref[:, h * NOPE:(h + 1) * NOPE], preferred_element_type=f32
        )


def combine(got, value):
    vmem = pl.BlockSpec(memory_space=pltpu.VMEM)
    return pl.pallas_call(
        combine_kernel,
        out_shape=jax.ShapeDtypeStruct((RDEV, HDEV * NOPE), f32),
        in_specs=[vmem, vmem],
        out_specs=vmem,
        scratch_shapes=[pltpu.VMEM((4, 64, 128), f32)],
        compiler_params=pltpu.CompilerParams(vmem_limit_bytes=24 * 1024 * 1024),
        name="combine",
    )(got, value)


def rotary_tables(lengths):
    half = ROPE // 2
    rates = 10000.0 ** (-jnp.arange(half, dtype=f32) / half)
    angles = lengths.astype(f32)[:, None] * rates
    cosine, sine = jnp.cos(angles), jnp.sin(angles)
    cos = jnp.tile(jnp.concatenate([cosine, cosine], axis=1), (1, HDEV))
    sin = jnp.tile(jnp.concatenate([-sine, sine], axis=1), (1, HDEV))
    return cos, sin


def canonical(blocks, axis, index):
    for bit in range(len(blocks).bit_length() - 1):
        flip = (index >> bit) & 1 == 1
        blocks = [jnp.where(flip, blocks[j ^ (1 << bit)], blocks[j]) for j in range(len(blocks))]
    return jnp.stack(blocks, axis=axis)


def swapped_out_weight(out_weight, core, z):
    cols = out_weight.shape[1]
    rows = out_weight.T.reshape(cols, 2, 4, 2, HDEV * NOPE)
    keep = lax.dynamic_index_in_dim(rows, core, 3, keepdims=False)
    send = lax.dynamic_index_in_dim(rows, 1 - core, 3, keepdims=False)
    pair = jnp.stack([keep, swap(send, "attn", 1)])
    out = [None] * 4
    out[0] = lax.dynamic_index_in_dim(pair, z, 3, keepdims=False)
    for j, mask in ((1, 2), (3, 6), (2, 4)):
        out[j] = swap(lax.dynamic_index_in_dim(pair, z ^ j, 3, keepdims=False), "attn", mask)
    return out


def on_device(
    c_query, up_query, rope_query, key_up, value_up, out_weight, cache, new_entry, lengths
):
    section = lax.axis_index("section")
    yh, z, core = (lax.axis_index(n) for n in ATTN)
    attn = yh * 8 + z * 2 + core
    span = cache.shape[1]

    with jax.named_scope("weights"):
        keys = [key_up]
        for mask in (1, 2, 6):
            keys = keys + [None] * len(keys)
            half = len(keys) // 2
            got = swap(jnp.stack(keys[:half]), "section", mask)
            for j in range(half):
                keys[half + j] = got[j]
        offsets = [0, 1, 2, 3, 6, 7, 4, 5]
        place_of = jnp.array([offsets.index(j) for j in range(8)], jnp.int32)
        order = place_of[section ^ jnp.arange(8, dtype=jnp.int32)]
        key_blocks = jnp.stack(keys)
        value = lax.all_gather(value_up, "section", axis=0, tiled=True)
        weight = swapped_out_weight(out_weight, core, z)
        cos, sin = rotary_tables(lengths)
        up = jnp.concatenate([up_query, rope_query], axis=1)

    with jax.named_scope("queries"):
        rows = exchange(
            jnp.transpose(c_query.reshape(RDEV, 8, -1), (1, 0, 2)), ("section",)
        ).reshape(64, -1)
        part = jnp.dot(rows, up, preferred_element_type=f32).reshape(8, RDEV, -1)
        parts = exchange(part, ("section",))
        queries = make_queries(order, parts, key_blocks, cos, sin)
        qa = exchange(jnp.broadcast_to(queries[None], (8,) + queries.shape), ("yh", "z"))
        qb = swap(qa, "attn", 1)

    with jax.named_scope("attention"):
        place = jnp.stack([attn * span, (attn == 0).astype(jnp.int32)])
        keep, send = attend(lengths, place, qa, qb, cache, new_entry[:, None, :].astype(f32))
        merged = merge(keep, swap(send, "attn", 1))
        got = exchange(merged, ("yh", "z"))

    with jax.named_scope("output"):
        mid = combine(got, value).astype(bf16)
        mids = exchange(jnp.broadcast_to(mid[None], (16,) + mid.shape), ("section", "yh"))
        mids = jnp.transpose(mids.reshape(8, 2, RDEV, -1), (0, 2, 1, 3)).reshape(64, 2, -1)
        outs = [
            lax.dot_general(
                mids, w, (((1, 2), (2, 3)), ((), ())), preferred_element_type=f32
            )
            for w in weight
        ]
        outs = [jnp.stack([o[:, 0], o[:, 1]], 1) for o in outs]
        outs = canonical(outs, 1, z)
        outs = canonical([outs[:, :, 0], outs[:, :, 1]], 2, core)
        share = exchange(outs.reshape(8, RDEV, -1), ("z", "core"))
        mixed = jnp.sum(share, axis=0).astype(bf16)
        return lax.ppermute(
            mixed,
            ALL,
            [
                (s * 16 + y * 8 + t, t * 16 + s * 2 + y)
                for s in range(8)
                for y in range(2)
                for t in range(8)
            ],
        )


def solution(mesh):
    split = Mesh(mesh.devices.reshape(8, 2, 4, 2), ALL)
    return jax.shard_map(
        on_device,
        mesh=split,
        in_specs=(
            P("section", None),
            P("section", ATTN),
            P("section", ATTN),
            P("section", ATTN),
            P("section", ATTN),
            P(None, ALL),
            P("section", ATTN, None),
            P("section", None),
            P("section"),
        ),
        out_specs=P("section", ATTN),
        check_vma=False,
    )
```

time: 708 us -> 168 us (0.24)
  waiting for transfers between devices: 557 us -> 50.8 us
  matrix products: 50.4 us -> 5.06 us
  starting transfers between devices: 13.7 us -> 45.4 us
  blocking collectives: 34 us -> 8.14 us
  Pallas kernels: 0 us -> 9.64 us
    all_gather x6 -> x1, waiting for transfers between devices: 406 us -> 0.01 us  [on_device(): value = lax.all_gather(value_up, 'section', axis=0, tiled=True)]
    unnamed x8 -> x1, waiting for transfers between devices: 81.8 us -> 0.68 us
    all_to_all x3 -> x5, waiting for transfers between devices: 68.9 us -> 22.5 us  [exchange(): return lax.all_to_all(x, names, 0, 0, tiled=True)]
    dot_general x6 -> x5, matrix products: 50.4 us -> 5.06 us  [the longest x4 4.09 us: on_device(): lax.dot_general(mids, w, (((1, 2), (2, 3)), ((), ())), preferred_element_...]
    ppermute x0 -> x10, waiting for transfers between devices: none -> 27.6 us  [the longest x9 21.3 us: swap(): return lax.ppermute(x, names, [(i, i ^ mask) for i in range(size)])]
    all_to_all x1, blocking collectives: 34 us -> 8.14 us  [exchange(): return lax.all_to_all(x, names, 0, 0, tiled=True)]
    all_gather x4 -> x0, local copies, waits for them, and re-layouts: 25.3 us -> none  [the longest x1 18.4 us: on_device(): owned_rows = lax.all_gather(swapped, 'section', axis=1, tiled=True)]
    ppermute x0 -> x10, starting transfers between devices: none -> 17.3 us  [the longest x9 12.9 us: swap(): return lax.ppermute(x, names, [(i, i ^ mask) for i in range(size)])]
  transfers between devices with their start and end apart: 10 -> 16, of which waited for: 9 -> 11; matrix products, arithmetic and copies ran while one was open for 3% -> 19% of each run, Pallas kernels for 0% -> 5%
where the time goes in v1:
time: 168 us; the launch traced here: 167 us
  waiting for transfers between devices  50.8 us (30%)
  starting transfers between devices  45.4 us (27%)
  local copies, waits for them, and re-layouts  29.7 us (18%)
  between operations  13.6 us (8%)
  Pallas kernels  9.64 us (6%)
  blocking collectives  8.14 us (5%)
  matrix products  5.06 us (3%)
  other arithmetic  4.31 us (3%)
    all_to_all x5, starting transfers between devices, exchange(): return lax.all_to_all(x, names, 0, 0, tiled=True)  28 us
    all_to_all x5, waiting for transfers between devices, exchange(): return lax.all_to_all(x, names, 0, 0, tiled=True)  22.5 us
    ppermute x9, waiting for transfers between devices, swap(): return lax.ppermute(x, names, [(i, i ^ mask) for i in range(size)])  21.3 us
    ppermute x9, starting transfers between devices, swap(): return lax.ppermute(x, names, [(i, i ^ mask) for i in range(size)])  12.9 us
    unnamed x20, local copies, waits for them, and re-layouts  12.1 us
    all_to_all x1, blocking collectives, exchange(): return lax.all_to_all(x, names, 0, 0, tiled=True)  8.14 us
    dynamic_slice x2, local copies, waits for them, and re-layouts, swapped_out_weight(): send = lax.dynamic_index_in_dim(rows, 1 - core, 3, keepdims=False)  7.64 us
    ppermute x1, waiting for transfers between devices, on_device(): lax.ppermute(mixed, ALL, [(s * 16 + y * 8 + t, t * 16 + s * 2 + y) for s...  6.28 us
  transfers between devices with their start and end apart: 16, of which 11 were waited for; matrix products, arithmetic and copies ran while one was open for 19% of the time, Pallas kernels for 5%

profile of v1, /device:TPU:7, one launch (start us, length us, event | category | flops | bytes accessed | tf_op | source)
XLA Modules:
  0.0 166.7 jit_solution(13664345918680988600)
XLA Ops:
  6.5 1.3 collective-permute-start
  7.8 3.3 %collective-permute-done = bf16[1,64,1024]{2,1,0:T(8,128)(2,1)S(1)} collective-permute-done((bf16[1,64,1024]{2,1,0:T(8,128)(2,1)}, bf16[1,64,1024]{2,1,0:T(8,128)(2,1)S(1)}, u32[]{:S(2)}, u32[]{:S(2)}) %collective-permute-start) | collective-permute-done | bytes 131104 | tf_op jit(solution)/shard_map/weights/ppermute | solution.py:29
  11.1 0.9 pad_maximum_fusion.2
  12.1 0.6 collective-permute-start.1
  12.7 0.8 reshape.57
  13.5 0.6 copy.25
  14.1 5.7 %all-to-all-start = ((bf16[8,8,192]{2,1,0:T(8,128)(2,1)}), bf16[8,8,192]{2,1,0:T(8,128)(2,1)S(1)}, u32[]{:S(2)}, u32[]{:S(2)}) async-start(bf16[8,8,192]{2,1,0:T(8,128)(2,1)} %copy.25), calls=%async_computation | async-start | bytes 65536 | tf_op jit(solution)/shard_map/queries/all_to_all | solution.py:33
  19.9 0.7 convert_element_type.15
  20.5 0.0 collective-permute-done.1
  20.5 1.0 pad_maximum_fusion.1
  21.5 0.1 collective-permute-start.2
  21.6 0.1 fusion.22
  21.7 0.1 pad_maximum_fusion.5
  21.8 0.1 tile.21.sin_ref
  21.9 0.1 tile.9.cos_ref
  22.0 1.2 all-to-all-done
  23.2 1.0 convolution_bitcast_fusion
  24.1 5.2 %all-to-all-start.1 = ((f32[8,8,1536]{2,1,0:T(8,128)}), f32[8,8,1536]{2,1,0:T(8,128)S(1)}, u32[]{:S(2)}, u32[]{:S(2)}) async-start(f32[8,8,1536]{2,1,0:T(8,128)} %convolution_bitcast_fusion), calls=%async_computation.1 | async-start | bytes 786432 | tf_op jit(solution)/shard_map/queries/all_to_all | solution.py:33
  29.3 0.6 gather_fusion
  30.0 4.9 %collective-permute-done.2 = bf16[4,64,1024]{2,1,0:T(8,128)(2,1)S(1)} collective-permute-done((bf16[4,64,1024]{2,1,0:T(8,128)(2,1)S(1)}, bf16[4,64,1024]{2,1,0:T(8,128)(2,1)S(1)}, u32[]{:S(2)}, u32[]{:S(2)}) %collective-permute-start.2) | collective-permute-done | bytes 524320 | tf_op jit(solution)/shard_map/weights/ppermute | solution.py:29
  34.9 0.1 pad_maximum_fusion.key_ref
  35.0 3.7 %all-to-all-done.1.part_ref = f32[8,8,1536]{2,1,0:T(8,128)S(1)} async-done(((f32[8,8,1536]{2,1,0:T(8,128)}), f32[8,8,1536]{2,1,0:T(8,128)S(1)}, u32[]{:S(2)}, u32[]{:S(2)}) %all-to-all-start.1) | async-done | bytes 393248 | tf_op jit(solution)/shard_map/queries/all_to_all | solution.py:33
  38.7 1.0 make_queries.1
  39.7 0.9 broadcast_in_dim.4
  40.6 7.4 %all-to-all-start.2 = ((bf16[8,64,576]{2,1,0:T(8,128)(2,1)}), bf16[8,64,576]{2,1,0:T(8,128)(2,1)S(1)}, u32[]{:S(2)}, u32[]{:S(2)}) async-start(bf16[8,64,576]{2,1,0:T(8,128)(2,1)} %broadcast_in_dim.4), calls=%async_computation.2 | async-start | bytes 1310720 | tf_op jit(solution)/shard_map/queries/all_to_all | solution.py:33
  48.0 0.0 all-gather.2.cloned.1.call-start
  48.0 0.7 all-gather.2.cloned.1.call-update
  48.7 8.6 %all-to-all-done.2.qa_ref = bf16[8,64,576]{2,1,0:T(8,128)(2,1)S(1)} async-done(((bf16[8,64,576]{2,1,0:T(8,128)(2,1)}), bf16[8,64,576]{2,1,0:T(8,128)(2,1)S(1)}, u32[]{:S(2)}, u32[]{:S(2)}) %all-to-all-start.2) | async-done | bytes 589856 | tf_op jit(solution)/shard_map/queries/all_to_all | solution.py:33
  57.3 4.9 %collective-permute-start.3 = (bf16[8,64,576]{2,1,0:T(8,128)(2,1)S(1)}, bf16[8,64,576]{2,1,0:T(8,128)(2,1)S(1)}, u32[]{:S(2)}, u32[]{:S(2)}) collective-permute-start(bf16[8,64,576]{2,1,0:T(8,128)(2,1)S(1)} %all-to-all-done.2.qa_ref), channel_id=1, source_target_pairs={{0,1},{1,0},{2,3},{3,2},{4,5},{5,4},{6,7},{7,6},{8,9},{9,8},{10,11... | collective-permute-start | bytes 1769480 | tf_op jit(solution)/shard_map/queries/ppermute | solution.py:29
  62.2 4.6 %reshape.62 = bf16[56,2,4,2,1024]{4,3,2,1,0:T(2,128)(2,1)S(1)} reshape(bf16[56,16384]{1,0:T(8,128)(2,1)} %bitcast.81) | data formatting | bytes 3670016 | tf_op jit(solution)/shard_map/weights/reshape | solution.py:265
  66.7 5.7 %constant_dynamic-slice_fusion = (bf16[56,2,4,1,1024]{4,3,2,1,0:T(2,128)(2,1)S(1)}, bf16[56,2,4,1,1024]{4,3,2,1,0:T(2,128)(2,1)}) fusion(bf16[56,2,4,2,1024]{4,3,2,1,0:T(2,128)(2,1)S(1)} %reshape.62, s32[]{:T(128)S(6)} %select_n.87, s32[]{:T(128)S(6)} %select_n.86), kind=kLoop, calls=%fused_computation.58 | loop fusion | bytes 3670024 | tf_op jit(solution)/shard_map/weights/jit(dynamic_index_in_dim)/dynamic_slice | solution.py:267
  72.5 1.9 %copy.55 = bf16[56,2,4,1,1024]{4,0,1,2,3:T(8,128)(2,1)} copy(bf16[56,2,4,1,1024]{4,3,2,1,0:T(2,128)(2,1)S(1)} %get-tuple-element.12) | data formatting | bytes 1835008 | tf_op jit(solution)/shard_map/weights/jit(dynamic_index_in_dim)/dynamic_slice | solution.py:267
  74.4 0.0 collective-permute-start.5
  74.4 0.1 pad_add_fusion.at_ref
  74.5 7.7 %copy.26.cache_ref = bf16[8,512,576]{2,1,0:T(8,128)(2,1)} copy(bf16[8,512,576]{1,2,0:T(8,128)(2,1)} %param.16) | data formatting | bytes 9437184 | tf_op args[6]
  82.2 2.5 %copy-done = bf16[8,512,576]{2,1,0:T(8,128)(2,1)S(1)} copy-done((bf16[8,512,576]{2,1,0:T(8,128)(2,1)S(1)}, bf16[8,512,576]{2,1,0:T(8,128)(2,1)}, u32[]{:S(2)}) %copy-start) | copy-done | bytes 4718616
  84.7 5.4 %attend.1 = (f32[8,64,640]{2,1,0:T(8,128)S(1)}, bf16[8,64,640]{2,1,0:T(8,128)(2,1)S(1)}) custom-call(s32[8]{0:T(128)S(1)} %copy-done.2, s32[2]{0:T(128)S(1)} %pad_add_fusion.at_ref, bf16[8,64,576]{2,1,0:T(8,128)(2,1)S(1)} %all-to-all-done.2.qa_ref, bf16[8,64,576]{2,1,0:T(8,128)(2,1)S(1)} %collective-permute-done.3.qb_ref, bf16[8,512,576]{2,1,0:T(8,128)(2,1)S(1)} %copy-done, ...), custom_call_target="tpu_custom_call" | custom-call | tf_op jit(solution)/shard_map/attention/attend/pallas_call | solution.py:171
  90.1 0.8 collective-permute-start.4
  90.9 1.7 %collective-permute-done.4.got_ref = bf16[8,64,640]{2,1,0:T(8,128)(2,1)S(1)} collective-permute-done((bf16[8,64,640]{2,1,0:T(8,128)(2,1)S(1)}, bf16[8,64,640]{2,1,0:T(8,128)(2,1)S(1)}, u32[]{:S(2)}, u32[]{:S(2)}) %collective-permute-start.4) | collective-permute-done | bytes 655392 | tf_op jit(solution)/shard_map/attention/ppermute | solution.py:29
  92.6 2.6 %merge.1 = bf16[8,64,640]{2,1,0:T(8,128)(2,1)} custom-call(f32[8,64,640]{2,1,0:T(8,128)S(1)} %get-tuple-element.7.keep_ref, bf16[8,64,640]{2,1,0:T(8,128)(2,1)S(1)} %collective-permute-done.4.got_ref), custom_call_target="tpu_custom_call" | custom-call | tf_op jit(solution)/shard_map/attention/merge/pallas_call | solution.py:198
  95.2 3.5 %all-to-all-start.3 = ((bf16[8,64,640]{2,1,0:T(8,128)(2,1)}), bf16[8,64,640]{2,1,0:T(8,128)(2,1)S(1)}, u32[]{:S(2)}, u32[]{:S(2)}) async-start(bf16[8,64,640]{2,1,0:T(8,128)(2,1)} %merge.1), calls=%async_computation.3 | async-start | bytes 1310720 | tf_op jit(solution)/shard_map/attention/all_to_all | solution.py:33
  98.8 1.0 copy.56
  99.8 1.3 fusion.11
  101.1 1.4 collective-permute-start.8
  102.5 2.4 %collective-permute-start.7 = (bf16[2,56,2,1024]{3,1,2,0:T(8,128)(2,1)S(1)}, bf16[2,56,2,1024]{3,1,2,0:T(8,128)(2,1)}, u32[]{:S(2)}, u32[]{:S(2)}) collective-permute-start(bf16[2,56,2,1024]{3,1,2,0:T(8,128)(2,1)S(1)} %get-tuple-element.11), channel_id=1, source_target_pairs={{0,4},{1,5},{2,6},{3,7},{4,0},{5,1},{6,2},{7,3},{8,12},{9,13},{10,... | collective-permute-start | bytes 1376264 | tf_op jit(solution)/shard_map/weights/ppermute | solution.py:29
  104.9 4.8 %all-to-all-done.3.got_ref = bf16[8,64,640]{2,1,0:T(8,128)(2,1)S(1)} async-done(((bf16[8,64,640]{2,1,0:T(8,128)(2,1)}), bf16[8,64,640]{2,1,0:T(8,128)(2,1)S(1)}, u32[]{:S(2)}, u32[]{:S(2)}) %all-to-all-start.3) | async-done | bytes 655392 | tf_op jit(solution)/shard_map/attention/all_to_all | solution.py:33
  109.7 1.2 copy-done.1
  110.9 0.7 combine.1
  111.6 0.7 broadcast_in_dim.5
  112.3 6.2 %all-to-all-start.4 = ((bf16[16,8,1024]{2,1,0:T(8,128)(2,1)}), bf16[16,8,1024]{2,1,0:T(8,128)(2,1)S(1)}, u32[]{:S(2)}, u32[]{:S(2)}) async-start(bf16[16,8,1024]{2,1,0:T(8,128)(2,1)} %broadcast_in_dim.5), calls=%async_computation.4 | async-start | bytes 524288 | tf_op jit(solution)/shard_map/output/all_to_all | solution.py:33
  118.5 1.4 collective-permute-start.6
  119.9 4.3 %all-to-all-done.4 = bf16[16,8,1024]{2,1,0:T(8,128)(2,1)S(1)} async-done(((bf16[16,8,1024]{2,1,0:T(8,128)(2,1)}), bf16[16,8,1024]{2,1,0:T(8,128)(2,1)S(1)}, u32[]{:S(2)}, u32[]{:S(2)}) %all-to-all-start.4) | async-done | bytes 262176 | tf_op jit(solution)/shard_map/output/all_to_all | solution.py:33
  124.2 1.3 convolution_bitcast_fusion.2
  125.5 4.0 %collective-permute-done.7 = bf16[2,56,2,1024]{3,1,2,0:T(8,128)(2,1)} collective-permute-done((bf16[2,56,2,1024]{3,1,2,0:T(8,128)(2,1)S(1)}, bf16[2,56,2,1024]{3,1,2,0:T(8,128)(2,1)}, u32[]{:S(2)}, u32[]{:S(2)}) %collective-permute-start.7) | collective-permute-done | bytes 458784 | tf_op jit(solution)/shard_map/weights/ppermute | solution.py:29
  129.5 1.3 convolution_bitcast_fusion.3
  130.8 1.2 convolution_bitcast_fusion.1
  132.0 7.5 %collective-permute-done.6 = bf16[2,56,2,1024]{3,1,2,0:T(8,128)(2,1)S(1)} collective-permute-done((bf16[2,56,2,1024]{3,1,2,0:T(8,128)(2,1)S(1)}, bf16[2,56,2,1024]{3,1,2,0:T(8,128)(2,1)S(1)}, u32[]{:S(2)}, u32[]{:S(2)}) %collective-permute-start.6) | collective-permute-done | bytes 458784 | tf_op jit(solution)/shard_map/weights/ppermute | solution.py:29
  139.5 0.3 select_bitcast_fusion.3
  139.9 0.2 copy.30
  140.1 0.3 reshape.63
  140.4 8.1 %all_to_all.30 = f32[8,8,448]{2,1,0:T(8,128)S(1)} all-to-all(f32[8,8,448]{2,1,0:T(8,128)S(1)} %reshape.63), channel_id=1, replica_groups=mesh['section'=8,'yh'=2,'z'=4,'core'=2] {'z','core'}, dimensions={0} | all-to-all | bytes 229376 | tf_op jit(solution)/shard_map/output/all_to_all | solution.py:33
  148.5 4.4 %collective-permute-start.9 = (bf16[8,448]{1,0:T(8,128)(2,1)S(1)}, bf16[8,448]{1,0:T(8,128)(2,1)S(1)}, u32[]{:S(2)}, u32[]{:S(2)}) collective-permute-start(bf16[8,448]{1,0:T(8,128)(2,1)S(1)} %reduce_sum.9), channel_id=1, source_target_pairs={{0,0},{1,16},{2,32},{3,48},{4,64},{5,80},{6,96},{7,112},{8,1},{9,1... | collective-permute-start | bytes 21512 | tf_op jit(solution)/shard_map/output/ppermute | solution.py:332
  153.0 6.3 %collective-permute-done.9 = bf16[8,448]{1,0:T(8,128)(2,1)S(1)} collective-permute-done((bf16[8,448]{1,0:T(8,128)(2,1)S(1)}, bf16[8,448]{1,0:T(8,128)(2,1)S(1)}, u32[]{:S(2)}, u32[]{:S(2)}) %collective-permute-start.9) | collective-permute-done | bytes 7200 | tf_op jit(solution)/shard_map/output/ppermute | solution.py:332
  159.2 0.6 copy.58
  (31 shorter events, 0.2 us)
Async XLA Ops:
  6.5 16.6 %copy-start.6 = (bf16[192,1024]{1,0:T(8,128)(2,1)S(1)}, bf16[192,1024]{1,0:T(8,128)(2,1)}, u32[]{:S(2)}) copy-start(bf16[192,1024]{1,0:T(8,128)(2,1)} %param.11) | copy-start | bytes 1179652
  6.5 16.6 %copy-start.7 = (bf16[192,512]{1,0:T(8,128)(2,1)S(1)}, bf16[192,512]{1,0:T(8,128)(2,1)}, u32[]{:S(2)}) copy-start(bf16[192,512]{1,0:T(8,128)(2,1)} %param.12) | copy-start | bytes 589828
  6.5 22.8 %copy-start.3 = (s32[8]{0:T(128)S(1)}, s32[8]{0:T(128)}, u32[]{:S(2)}) copy-start(s32[8]{0:T(128)} %constant.57.clone) | copy-start | bytes 100
  6.5 4.6 %collective-permute-start = (bf16[1,64,1024]{2,1,0:T(8,128)(2,1)}, bf16[1,64,1024]{2,1,0:T(8,128)(2,1)S(1)}, u32[]{:S(2)}, u32[]{:S(2)}) collective-permute-start(bf16[1,64,1024]{2,1,0:T(8,128)(2,1)} %bitcast.82), channel_id=1, source_target_pairs={{0,16},{16,0},{32,48},{48,32},{64,80},{80,64},{96,112},{112,96},{1... | collective-permute-start | bytes 393224 | tf_op jit(solution)/shard_map/weights/ppermute | solution.py:29
  12.1 8.5 %collective-permute-start.1 = (bf16[2,64,1024]{2,1,0:T(8,128)(2,1)S(1)}, bf16[2,64,1024]{2,1,0:T(8,128)(2,1)S(1)}, u32[]{:S(2)}, u32[]{:S(2)}) collective-permute-start(bf16[2,64,1024]{2,1,0:T(8,128)(2,1)S(1)} %pad_maximum_fusion.2), channel_id=1, source_target_pairs={{0,32},{16,48},{32,0},{48,16},{64,96},{80,112},{96,64},{112,80},{1... | collective-permute-start | bytes 786440 | tf_op jit(solution)/shard_map/weights/ppermute | solution.py:29
  14.1 20.7 %copy-start.5 = (bf16[64,1024]{1,0:T(8,128)(2,1)S(1)}, bf16[64,1024]{1,0:T(8,128)(2,1)}, u32[]{:S(2)}) copy-start(bf16[64,1024]{1,0:T(8,128)(2,1)} %param.13) | copy-start | bytes 393220
  14.1 9.0 %all-to-all-start = ((bf16[8,8,192]{2,1,0:T(8,128)(2,1)}), bf16[8,8,192]{2,1,0:T(8,128)(2,1)S(1)}, u32[]{:S(2)}, u32[]{:S(2)}) async-start(bf16[8,8,192]{2,1,0:T(8,128)(2,1)} %copy.25), calls=%async_computation | async-start | bytes 65536 | tf_op jit(solution)/shard_map/queries/all_to_all | solution.py:33
  21.5 13.4 %collective-permute-start.2 = (bf16[4,64,1024]{2,1,0:T(8,128)(2,1)S(1)}, bf16[4,64,1024]{2,1,0:T(8,128)(2,1)S(1)}, u32[]{:S(2)}, u32[]{:S(2)}) collective-permute-start(bf16[4,64,1024]{2,1,0:T(8,128)(2,1)S(1)} %pad_maximum_fusion.1), channel_id=1, source_target_pairs={{0,96},{16,112},{32,64},{48,80},{64,32},{80,48},{96,0},{112,16},{1... | collective-permute-start | bytes 1572872 | tf_op jit(solution)/shard_map/weights/ppermute | solution.py:29
  24.1 14.5 %all-to-all-start.1 = ((f32[8,8,1536]{2,1,0:T(8,128)}), f32[8,8,1536]{2,1,0:T(8,128)S(1)}, u32[]{:S(2)}, u32[]{:S(2)}) async-start(f32[8,8,1536]{2,1,0:T(8,128)} %convolution_bitcast_fusion), calls=%async_computation.1 | async-start | bytes 786432 | tf_op jit(solution)/shard_map/queries/all_to_all | solution.py:33
  40.6 16.7 %all-to-all-start.2 = ((bf16[8,64,576]{2,1,0:T(8,128)(2,1)}), bf16[8,64,576]{2,1,0:T(8,128)(2,1)S(1)}, u32[]{:S(2)}, u32[]{:S(2)}) async-start(bf16[8,64,576]{2,1,0:T(8,128)(2,1)} %broadcast_in_dim.4), calls=%async_computation.2 | async-start | bytes 1310720 | tf_op jit(solution)/shard_map/queries/all_to_all | solution.py:33
  48.0 56.9 %all-gather.2.cloned.1.call-start = ((), (), s32[]{:S(2)}) async-start(), calls=%async_computation.6 | async-start | bytes 1179648 | tf_op jit(solution)/shard_map/weights/all_gather | solution.py:296
  57.3 25.0 %collective-permute-start.3 = (bf16[8,64,576]{2,1,0:T(8,128)(2,1)S(1)}, bf16[8,64,576]{2,1,0:T(8,128)(2,1)S(1)}, u32[]{:S(2)}, u32[]{:S(2)}) collective-permute-start(bf16[8,64,576]{2,1,0:T(8,128)(2,1)S(1)} %all-to-all-done.2.qa_ref), channel_id=1, source_target_pairs={{0,1},{1,0},{2,3},{3,2},{4,5},{5,4},{6,7},{7,6},{8,9},{9,8},{10,11... | collective-permute-start | bytes 1769480 | tf_op jit(solution)/shard_map/queries/ppermute | solution.py:29
  74.4 25.4 %collective-permute-start.5 = (bf16[56,2,4,1024]{3,0,1,2:T(8,128)(2,1)}, bf16[56,2,4,1024]{3,0,1,2:T(8,128)(2,1)}, u32[]{:S(2)}, u32[]{:S(2)}) collective-permute-start(bf16[56,2,4,1024]{3,0,1,2:T(8,128)(2,1)} %bitcast.73), channel_id=1, source_target_pairs={{0,1},{1,0},{2,3},{3,2},{4,5},{5,4},{6,7},{7,6},{8,9},{9,8},{10,11... | collective-permute-start | bytes 2752520 | tf_op jit(solution)/shard_map/weights/ppermute | solution.py:29
  74.5 7.7 %copy-start.8 = (bf16[8,576]{1,0:T(8,128)(2,1)S(1)}, bf16[8,576]{1,0:T(8,128)(2,1)}, u32[]{:S(2)}) copy-start(bf16[8,576]{1,0:T(8,128)(2,1)} %param.17) | copy-start | bytes 27652
  74.5 7.8 %copy-start.2 = (s32[8]{0:T(128)S(1)}, s32[8]{0:T(128)}, u32[]{:S(2)}) copy-start(s32[8]{0:T(128)} %len_ref.1) | copy-start | bytes 100
  82.2 2.5 %copy-start = (bf16[8,512,576]{2,1,0:T(8,128)(2,1)S(1)}, bf16[8,512,576]{2,1,0:T(8,128)(2,1)}, u32[]{:S(2)}) copy-start(bf16[8,512,576]{2,1,0:T(8,128)(2,1)} %copy.26.cache_ref) | copy-start | bytes 14155780
  90.1 2.5 %collective-permute-start.4 = (bf16[8,64,640]{2,1,0:T(8,128)(2,1)S(1)}, bf16[8,64,640]{2,1,0:T(8,128)(2,1)S(1)}, u32[]{:S(2)}, u32[]{:S(2)}) collective-permute-start(bf16[8,64,640]{2,1,0:T(8,128)(2,1)S(1)} %get-tuple-element.8), channel_id=1, source_target_pairs={{0,1},{1,0},{2,3},{3,2},{4,5},{5,4},{6,7},{7,6},{8,9},{9,8},{10,11... | collective-permute-start | bytes 1966088 | tf_op jit(solution)/shard_map/attention/ppermute | solution.py:29
  92.6 6.1 %copy-start.4 = (bf16[56,2,4,1,1024]{4,3,2,1,0:T(2,128)(2,1)S(1)}, bf16[56,2,4,1,1024]{4,3,2,1,0:T(2,128)(2,1)}, u32[]{:S(2)}) copy-start(bf16[56,2,4,1,1024]{4,3,2,1,0:T(2,128)(2,1)} %get-tuple-element.13) | copy-start | bytes 2752516
  95.2 14.5 %all-to-all-start.3 = ((bf16[8,64,640]{2,1,0:T(8,128)(2,1)}), bf16[8,64,640]{2,1,0:T(8,128)(2,1)S(1)}, u32[]{:S(2)}, u32[]{:S(2)}) async-start(bf16[8,64,640]{2,1,0:T(8,128)(2,1)} %merge.1), calls=%async_computation.3 | async-start | bytes 1310720 | tf_op jit(solution)/shard_map/attention/all_to_all | solution.py:33
  101.1 18.8 %collective-permute-start.8 = (bf16[2,56,2,1024]{3,1,2,0:T(8,128)(2,1)S(1)}, bf16[2,56,2,1024]{3,1,2,0:T(8,128)(2,1)}, u32[]{:S(2)}, u32[]{:S(2)}) collective-permute-start(bf16[2,56,2,1024]{3,1,2,0:T(8,128)(2,1)S(1)} %get-tuple-element.9), channel_id=1, source_target_pairs={{0,2},{1,3},{2,0},{3,1},{4,6},{5,7},{6,4},{7,5},{8,10},{9,11},{10,... | collective-permute-start | bytes 1376264 | tf_op jit(solution)/shard_map/weights/ppermute | solution.py:29
  102.5 27.0 %collective-permute-start.7 = (bf16[2,56,2,1024]{3,1,2,0:T(8,128)(2,1)S(1)}, bf16[2,56,2,1024]{3,1,2,0:T(8,128)(2,1)}, u32[]{:S(2)}, u32[]{:S(2)}) collective-permute-start(bf16[2,56,2,1024]{3,1,2,0:T(8,128)(2,1)S(1)} %get-tuple-element.11), channel_id=1, source_target_pairs={{0,4},{1,5},{2,6},{3,7},{4,0},{5,1},{6,2},{7,3},{8,12},{9,13},{10,... | collective-permute-start | bytes 1376264 | tf_op jit(solution)/shard_map/weights/ppermute | solution.py:29
  109.7 1.2 copy-start.1
  112.3 11.9 %all-to-all-start.4 = ((bf16[16,8,1024]{2,1,0:T(8,128)(2,1)}), bf16[16,8,1024]{2,1,0:T(8,128)(2,1)S(1)}, u32[]{:S(2)}, u32[]{:S(2)}) async-start(bf16[16,8,1024]{2,1,0:T(8,128)(2,1)} %broadcast_in_dim.5), calls=%async_computation.4 | async-start | bytes 524288 | tf_op jit(solution)/shard_map/output/all_to_all | solution.py:33
  118.5 21.0 %collective-permute-start.6 = (bf16[2,56,2,1024]{3,1,2,0:T(8,128)(2,1)S(1)}, bf16[2,56,2,1024]{3,1,2,0:T(8,128)(2,1)S(1)}, u32[]{:S(2)}, u32[]{:S(2)}) collective-permute-start(bf16[2,56,2,1024]{3,1,2,0:T(8,128)(2,1)S(1)} %get-tuple-element.10), channel_id=1, source_target_pairs={{0,6},{1,7},{2,4},{3,5},{4,2},{5,3},{6,0},{7,1},{8,14},{9,15},{10,... | collective-permute-start | bytes 1376264 | tf_op jit(solution)/shard_map/weights/ppermute | solution.py:29
  148.5 10.7 %collective-permute-start.9 = (bf16[8,448]{1,0:T(8,128)(2,1)S(1)}, bf16[8,448]{1,0:T(8,128)(2,1)S(1)}, u32[]{:S(2)}, u32[]{:S(2)}) collective-permute-start(bf16[8,448]{1,0:T(8,128)(2,1)S(1)} %reduce_sum.9), channel_id=1, source_target_pairs={{0,0},{1,16},{2,32},{3,48},{4,64},{5,80},{6,96},{7,112},{8,1},{9,1... | collective-permute-start | bytes 21512 | tf_op jit(solution)/shard_map/output/ppermute | solution.py:332
Sparse Core Ops, SparseCore 0:
  50.4 37.6 all-gather.1

commit v2 on v0

v2 whole, which is shorter than its diff:
```python
import functools

import jax
import jax.numpy as jnp
from jax import lax
from jax.experimental import pallas as pl
from jax.experimental.pallas import tpu as pltpu
from jax.sharding import Mesh
from jax.sharding import PartitionSpec as P

KL = 512
NOPE = 128
ROPE = 64
QDIM = KL + ROPE
SLICE = 192
PACK = KL + 128
ROWS = 64
SCALE = (NOPE + ROPE) ** -0.5
NEG = -1e30

ATTN = ("yh", "z", "core")
ALL = ("section",) + ATTN
bf16 = jnp.bfloat16
f32 = jnp.float32

VMEM = pl.BlockSpec(memory_space=pltpu.VMEM)
SMEM = pl.BlockSpec(memory_space=pltpu.SMEM)
ANY = pl.BlockSpec(memory_space=pl.ANY)
HBM = pl.BlockSpec(memory_space=pltpu.HBM)
NT = (((1,), (1,)), ((), ()))


def swap(x, mask):
    return lax.ppermute(x, ATTN, [(i, i ^ mask) for i in range(16)])


def exchange(x, names):
    return lax.all_to_all(x, names, 0, 0, tiled=True)


def call(kernel, out_shape, in_specs, args, scratch=(), out_specs=None, limit=32):
    if out_specs is None:
        out_specs = jax.tree.map(lambda _: VMEM, out_shape)
    return pl.pallas_call(
        kernel,
        out_shape=out_shape,
        in_specs=in_specs,
        out_specs=out_specs,
        scratch_shapes=list(scratch),
        compiler_params=pltpu.CompilerParams(vmem_limit_bytes=limit * 1024 * 1024),
        name=kernel.__name__,
    )(*args)


def shaped(dtype, *shape):
    return jax.ShapeDtypeStruct(shape, dtype)


def pack_stats(top, mass):
    lane = lax.broadcasted_iota(jnp.int32, top.shape, 1)
    out = jnp.zeros(top.shape, f32)
    for start, value in ((0, top), (3, mass)):
        for i in range(3):
            term = value.astype(bf16).astype(f32)
            out = jnp.where(lane == start + i, term, out)
            value = value - term
    return out


def unpack_stats(packed):
    row = lax.broadcasted_iota(jnp.int32, (128, 256), 0)
    col = lax.broadcasted_iota(jnp.int32, (128, 256), 1)
    low = jnp.where(col < 128, 0, 3)
    pick = jnp.where((row >= low) & (row < low + 3), 1.0, 0.0).astype(bf16)
    both = jnp.dot(packed, pick, preferred_element_type=f32)
    return both[:, :128], both[:, 128:]


def widen(x):
    return jnp.concatenate([x] * (KL // 128), axis=1)


def blocks_kernel(at_ref, weight_ref, *refs):
    outs, sems = refs[:4], refs[4]
    copies = []
    for j in range(4):
        for c in range(2):
            for y in range(2):
                start = pl.multiple_of((y * 8 + (at_ref[0] ^ j) * 2 + c) * 1024, 1024)
                copies.append(
                    pltpu.make_async_copy(
                        weight_ref.at[:, pl.ds(start, 1024)],
                        outs[j].at[c, y],
                        sems.at[j * 4 + c * 2 + y],
                    )
                )
    for copy in copies:
        copy.start()
    for copy in copies:
        copy.wait()


def pick_kernel(at_ref, *refs):
    pieces, out_ref, sems = refs[:4], refs[4], refs[5]
    copies = [
        pltpu.make_async_copy(pieces[j].at[1 - at_ref[1]], out_ref.at[j], sems.at[j])
        for j in range(4)
    ]
    for copy in copies:
        copy.start()
    for copy in copies:
        copy.wait()


def slices_kernel(length_ref, query_ref, key_ref, value_ref, early_ref, out_ref, query_scr, sems):
    copies = [pltpu.make_async_copy(query_ref, query_scr, sems.at[16])]
    for j in range(8):
        cols = pl.ds(j * 128, 128)
        for i, ref in enumerate((key_ref, value_ref)):
            copies.append(
                pltpu.make_async_copy(
                    ref.at[:, cols], out_ref.at[j, pl.ds(i * 64, 64), :], sems.at[j * 2 + i]
                )
            )
    for copy in copies:
        copy.start()
    lane = lax.broadcasted_iota(jnp.int32, (8, ROPE), 1)
    row = lax.broadcasted_iota(jnp.int32, (8, ROPE), 0)
    length = jnp.zeros((8, ROPE), jnp.int32)
    for r in range(8):
        length = jnp.where(row == r, length_ref[r], length)
    length = length.astype(f32)
    high = length.astype(bf16).astype(f32)
    tail = jnp.where(lane == 0, high, jnp.where(lane == 1, length - high, 0.0))
    copies[0].wait()
    query = query_scr[...].astype(f32)
    for j in range(8):
        piece = query[:, j * SLICE:(j + 1) * SLICE]
        rest = jnp.concatenate([piece[:, 128:], tail], axis=1)
        out_ref[j, 128:144, :] = jnp.concatenate([piece[:, :128], rest], axis=0).astype(bf16)
    for copy in copies[1:]:
        copy.wait()


def partial_kernel(got_ref, up_hbm, rope_hbm, out_ref, up_ref, rope_ref, sems):
    copies = [
        pltpu.make_async_copy(up_hbm, up_ref, sems.at[0]),
        pltpu.make_async_copy(rope_hbm, rope_ref, sems.at[1]),
    ]
    for copy in copies:
        copy.start()
    tiles = [got_ref[t, 128:144, :].astype(f32) for t in range(8)]
    rows = jnp.concatenate(
        [
            jnp.concatenate([x[0:8] for x in tiles], axis=0),
            jnp.concatenate([x[8:16] for x in tiles], axis=0)[:, :ROPE],
        ],
        axis=1,
    ).astype(bf16)
    for copy in copies:
        copy.wait()
    nope = jnp.dot(rows, up_ref[...], preferred_element_type=f32)
    rope = jnp.dot(rows, rope_ref[...], preferred_element_type=f32)
    for h in range(8):
        out_ref[h, :, 0:NOPE] = nope[:, h * NOPE:(h + 1) * NOPE]
        out_ref[h, :, NOPE:SLICE] = rope[:, h * ROPE:(h + 1) * ROPE]


def query_kernel(part_ref, got_ref, cos_ref, sin_ref, *refs):
    out_ref = refs[-1]
    q = part_ref[0]
    for i in range(1, 8):
        q = q + part_ref[i]
    nope = q[:, :NOPE]
    high = nope.astype(bf16).astype(f32)
    lhs = jnp.concatenate([high, nope - high], axis=0).astype(bf16)
    key = jnp.concatenate([got_ref[t, 0:64, :] for t in range(8)], axis=0)
    lat = lax.dot_general(lhs, key, NT, preferred_element_type=f32)
    lat = lat[:ROWS] + lat[ROWS:]
    a, b = q[:, NOPE:NOPE + ROPE // 2], q[:, NOPE + ROPE // 2:]
    cos, sin = cos_ref[...], sin_ref[...]
    rope = jnp.concatenate([a * cos - b * sin, a * sin + b * cos], axis=1)
    for s in range(8):
        at = slice(s * 8, s * 8 + 8)
        out_ref[s, :, 0:KL] = jnp.concatenate([lat[at]] * 8, axis=0).astype(bf16)
        out_ref[s, :, KL:QDIM] = jnp.concatenate([rope[at]] * 8, axis=0).astype(bf16)


def attend_kernel(len_ref, at_ref, qa_ref, qb_ref, cache_ref, new_ref, *refs):
    keep_ref, send_ref, q_scr, send_scr, cache_scr, sems = refs[-6:]
    copies = [
        pltpu.make_async_copy(cache_ref.at[r], cache_scr.at[r], sems.at[r]) for r in range(8)
    ]
    for copy in copies:
        copy.start()
    for j in range(5):
        width = min(128, QDIM - j * 128)
        at = slice(j * 128, j * 128 + width)
        q_scr[j, 0:512, 0:width] = qa_ref[:, at].astype(f32)
        q_scr[j, 512:1024, 0:width] = qb_ref[:, at].astype(f32)
    first, mine = at_ref[0], at_ref[1] == 1
    news = new_ref[...].astype(f32)
    for r in range(8):
        heads = pl.ds(r, 128, stride=8)
        q = jnp.concatenate(
            [q_scr[j, heads, :] for j in range(4)] + [q_scr[4, heads, :][:, :ROPE]], axis=1
        )
        new = news[r:r + 1, :]
        own = jnp.sum(q * new, axis=1, keepdims=True) * SCALE
        copies[r].wait()
        score = jnp.dot(q.astype(bf16), cache_scr[r], preferred_element_type=f32) * SCALE
        slot = lax.broadcasted_iota(jnp.int32, score.shape, 1) + first
        valid = slot < len_ref[r]
        score = jnp.where(valid, score, NEG)
        top = jnp.max(score, axis=1, keepdims=True)
        prob = jnp.where(valid, jnp.exp(score - top), 0.0)
        mass = jnp.sum(prob, axis=1, keepdims=True)
        num = lax.dot_general(
            prob.astype(bf16), cache_scr[r, 0:KL, :], NT, preferred_element_type=f32
        )
        own = jnp.where(mine, own, NEG)
        best = jnp.maximum(top, own)
        scale_old = jnp.exp(top - best)
        scale_new = jnp.where(mine, jnp.exp(own - best), 0.0)
        num = num * scale_old + scale_new * new[:, :KL]
        mass = mass * scale_old + scale_new
        stats = pack_stats(
            jnp.broadcast_to(best, (128, 128)), jnp.broadcast_to(mass, (128, 128))
        )
        half = pl.ds(r, 64, stride=8)
        for j in range(5):
            tile = num[:, j * 128:(j + 1) * 128] if j < 4 else stats
            keep_ref[j, half, :] = tile[0:64]
            send_scr[j, half, :] = tile[64:128]
    for j in range(5):
        send_ref[:, j * 128:(j + 1) * 128] = send_scr[j].astype(bf16)


def merge_kernel(keep_ref, got_ref, out_ref):
    for i in range(8):
        at = slice(i * 64, i * 64 + 64)
        top_a, mass_a = unpack_stats(keep_ref[4, at, :].astype(bf16))
        top_b, mass_b = unpack_stats(got_ref[at, KL:PACK])
        best = jnp.maximum(top_a, top_b)
        wa, wb = jnp.exp(top_a - best), jnp.exp(top_b - best)
        for j in range(4):
            cols = slice(j * 128, j * 128 + 128)
            num = keep_ref[j, at, :] * wa + got_ref[at, cols].astype(f32) * wb
            out_ref[at, cols] = num.astype(bf16)
        out_ref[at, KL:PACK] = pack_stats(best, mass_a * wa + mass_b * wb).astype(bf16)


def combine_kernel(got_ref, first_ref, out_ref):
    value = jnp.concatenate([first_ref[t, 64:128, :] for t in range(8)], axis=0)
    latents = []
    for s in range(8):
        top, mass = unpack_stats(got_ref[s, :, KL:PACK])
        top = top.reshape(8, 8, 128)
        best = jnp.max(top, axis=0)
        w = jnp.exp(top - best[None])
        den = jnp.sum(mass.reshape(8, 8, 128) * w, axis=0)
        num = [
            jnp.sum(
                got_ref[s, :, j * 128:(j + 1) * 128].astype(f32).reshape(8, 8, 128) * w, axis=0
            )
            / den
            for j in range(4)
        ]
        latents.append(jnp.concatenate(num, axis=1))
    latent = jnp.concatenate(latents, axis=0).astype(bf16)
    mid = jnp.dot(latent, value, preferred_element_type=f32).astype(bf16)
    for i in range(16):
        out_ref[i] = mid


def project_kernel(at_ref, mid_ref, *refs):
    pieces, other_ref, out_ref = refs[:4], refs[4], refs[5]
    lhs = [
        jnp.concatenate([mid_ref[i * 2 + y] for i in range(8)], axis=1) for y in range(2)
    ]
    for j in range(4):
        tile = []
        for k in range(2):
            out = sum(
                lax.dot_general(
                    lhs[y],
                    other_ref[j, y] if k else pieces[j][at_ref[1], y],
                    NT,
                    preferred_element_type=f32,
                )
                for y in range(2)
            )
            tile += [out, jnp.zeros((ROWS, 8), f32)]
        out_ref[:, j * 128:(j + 1) * 128] = jnp.concatenate(tile, axis=1)


def total_kernel(share_ref, out_ref):
    total = [jnp.zeros((8, 128), f32) for _ in range(4)]
    for t in range(8):
        for k in range(4):
            tile = share_ref[t, :, (k ^ (t >> 1)) * 128:((k ^ (t >> 1)) + 1) * 128]
            if t & 1:
                tile = jnp.concatenate([tile[:, 64:], tile[:, :64]], axis=1)
            total[k] = total[k] + tile
    out_ref[...] = jnp.concatenate(
        [total[k // 2][:, (k % 2) * 64:(k % 2) * 64 + 56] for k in range(8)], axis=1
    ).astype(bf16)


def on_device(
    c_query, up_query, rope_query, key_up, value_up, out_weight, cache, new_entry, lengths
):
    yh, z, core = (lax.axis_index(n) for n in ATTN)
    attn = yh * 8 + z * 2 + core
    where = jnp.stack([z, core])
    span = cache.shape[1]

    with jax.named_scope("weights"):
        pieces = call(
            blocks_kernel,
            [shaped(bf16, 2, 2, 56, 1024)] * 4,
            [SMEM, HBM],
            (where, out_weight.T),
            [pltpu.SemaphoreType.DMA((16,))],
        )
        pieces = [p if j == 0 else swap(p, j * 2) for j, p in enumerate(pieces)]
        others = swap(
            call(
                pick_kernel,
                shaped(bf16, 4, 2, 56, 1024),
                [SMEM] + [ANY] * 4,
                (where, *pieces),
                [pltpu.SemaphoreType.DMA((4,))],
            ),
            1,
        )

    with jax.named_scope("queries"):
        slices = call(
            slices_kernel,
            shaped(bf16, 8, 144, 128),
            [SMEM] + [HBM] * 3 + [ANY],
            (lengths, c_query, key_up, value_up, pieces[0]),
            [pltpu.VMEM(c_query.shape, bf16), pltpu.SemaphoreType.DMA((17,))],
        )
        first = exchange(slices, ("section",))
        part = call(
            partial_kernel,
            shaped(f32, 8, ROWS, SLICE),
            [VMEM, HBM, HBM],
            (first, up_query, rope_query),
            [
                pltpu.VMEM(up_query.shape, bf16),
                pltpu.VMEM(rope_query.shape, bf16),
                pltpu.SemaphoreType.DMA((2,)),
            ],
        )
        parts = exchange(part, ("section",))
        position = (
            first[:, 136:144, ROPE].astype(f32) + first[:, 136:144, ROPE + 1].astype(f32)
        ).reshape(ROWS)
        half = ROPE // 2
        rates = 10000.0 ** (-jnp.arange(half, dtype=f32) / half)
        angles = position[:, None] * rates
        queries = call(
            query_kernel,
            shaped(bf16, 8, 64, QDIM),
            [VMEM] * 4 + [ANY] * 3,
            (parts, first, jnp.cos(angles), jnp.sin(angles), pieces[1], pieces[2], pieces[3]),
        )
        qa = exchange(queries.reshape(64, 8, QDIM), ("section", "yh", "z"))
        qb = swap(qa, 1)

    with jax.named_scope("attention"):
        place = jnp.stack([attn * span, (attn == 0).astype(jnp.int32)])
        keep, send = call(
            attend_kernel,
            [shaped(f32, 5, 512, 128), shaped(bf16, 512, PACK)],
            [SMEM, SMEM, VMEM, VMEM, HBM, VMEM],
            (
                lengths,
                place,
                qa.reshape(512, QDIM),
                qb.reshape(512, QDIM),
                jnp.swapaxes(cache, 1, 2),
                new_entry,
            ),
            [
                pltpu.VMEM((5, 1024, 128), f32),
                pltpu.VMEM((5, 512, 128), f32),
                pltpu.VMEM((8, QDIM, span), bf16),
                pltpu.SemaphoreType.DMA((8,)),
            ],
        )
        merged = call(merge_kernel, shaped(bf16, 512, PACK), [VMEM] * 2, (keep, swap(send, 1)))
        got = exchange(merged.reshape(64, 8, PACK), ("section", "yh", "z"))

    with jax.named_scope("output"):
        mid = call(
            combine_kernel,
            shaped(bf16, 16, ROWS, NOPE),
            [VMEM] * 2,
            (got.reshape(8, 64, PACK), first),
        )
        mids = exchange(mid, ("section", "yh"))
        outs = call(
            project_kernel,
            shaped(f32, ROWS, 512),
            [SMEM] + [VMEM] * 6,
            (where, mids, *pieces, others),
        )
        share = exchange(outs.reshape(8, 8, 512), ("z", "core"))
        mixed = call(total_kernel, shaped(bf16, 8, 448), [VMEM], (share,))
        return lax.ppermute(
            mixed,
            ALL,
            [
                (s * 16 + y * 8 + t, t * 16 + s * 2 + y)
                for s in range(8)
                for y in range(2)
                for t in range(8)
            ],
        )


def solution(mesh):
    split = Mesh(mesh.devices.reshape(8, 2, 4, 2), ALL)
    return jax.shard_map(
        on_device,
        mesh=split,
        in_specs=(
            P("section", None),
            P("section", ATTN),
            P("section", ATTN),
            P("section", ATTN),
            P("section", ATTN),
            P(None, ALL),
            P("section", ATTN, None),
            P("section", None),
            P("section"),
        ),
        out_specs=P("section", ATTN),
        check_vma=False,
    )
```

time: 708 us -> 127 us (0.18)
  waiting for transfers between devices: 557 us -> 26.2 us
  matrix products: 50.4 us -> 0 us
  local copies, waits for them, and re-layouts: 32.9 us -> 4.55 us
  Pallas kernels: 0 us -> 18.2 us
  starting transfers between devices: 13.7 us -> 30.2 us
  between operations: 13.7 us -> 0.16 us
  blocking collectives: 34 us -> 46.2 us
    all_gather x6 -> x0, waiting for transfers between devices: 406 us -> none  [the longest x1 238 us: on_device(): owned_rows = lax.all_gather(swapped, 'section', axis=1, tiled=True)]
    unnamed x8 -> x0, waiting for transfers between devices: 81.8 us -> none
    all_to_all x3, waiting for transfers between devices: 68.9 us -> 5.57 us  [exchange(): return lax.all_to_all(x, names, 0, 0, tiled=True)]
    dot_general x6 -> x0, matrix products: 50.4 us -> none  [the longest x1 34.3 us: on_device(): jnp.dot(latent_out.reshape(row_count, heads_dev * KL), absorbed_out.resha...]
    all_gather x4 -> x0, local copies, waits for them, and re-layouts: 25.3 us -> none  [the longest x1 18.4 us: on_device(): owned_rows = lax.all_gather(swapped, 'section', axis=1, tiled=True)]
    ppermute x0 -> x7, waiting for transfers between devices: none -> 20.7 us  [the longest x6 15.7 us: swap(): return lax.ppermute(x, ATTN, [(i, i ^ mask) for i in range(16)])]
    pallas_call x0 -> x10, Pallas kernels: none -> 18.2 us  [call(): pl.pallas_call(kernel, out_shape=out_shape, in_specs=in_specs, out_specs=...]
    ppermute x0 -> x7, starting transfers between devices: none -> 15.2 us  [the longest x6 9.55 us: swap(): return lax.ppermute(x, ATTN, [(i, i ^ mask) for i in range(16)])]
  transfers between devices with their start and end apart: 10 -> 10, of which waited for: 9 -> 5; matrix products, arithmetic and copies ran while one was open for 3% -> 0% of each run, Pallas kernels for 0% -> 4%
where the time goes in v2:
time: 127 us; the launch traced here: 126 us
  blocking collectives  46.2 us (36%)
  starting transfers between devices  30.2 us (24%)
  waiting for transfers between devices  26.2 us (21%)
  Pallas kernels  18.2 us (14%)
  local copies, waits for them, and re-layouts  4.55 us (4%)
    all_to_all x3, blocking collectives, exchange(): return lax.all_to_all(x, names, 0, 0, tiled=True)  46.2 us
    pallas_call x10, Pallas kernels, call(): pl.pallas_call(kernel, out_shape=out_shape, in_specs=in_specs, out_specs=...  18.2 us
    ppermute x6, waiting for transfers between devices, swap(): return lax.ppermute(x, ATTN, [(i, i ^ mask) for i in range(16)])  15.7 us
    all_to_all x3, starting transfers between devices, exchange(): return lax.all_to_all(x, names, 0, 0, tiled=True)  14.9 us
    ppermute x6, starting transfers between devices, swap(): return lax.ppermute(x, ATTN, [(i, i ^ mask) for i in range(16)])  9.55 us
    ppermute x1, starting transfers between devices, on_device(): lax.ppermute(mixed, ALL, [(s * 16 + y * 8 + t, t * 16 + s * 2 + y) for s...  5.69 us
    all_to_all x3, waiting for transfers between devices, exchange(): return lax.all_to_all(x, names, 0, 0, tiled=True)  5.57 us
    ppermute x1, waiting for transfers between devices, on_device(): lax.ppermute(mixed, ALL, [(s * 16 + y * 8 + t, t * 16 + s * 2 + y) for s...  5 us
  transfers between devices with their start and end apart: 10, of which 5 were waited for; matrix products, arithmetic and copies ran while one was open for 0% of the time, Pallas kernels for 4%

profile of v2, /device:TPU:7, one launch (start us, length us, event | category | flops | bytes accessed | tf_op | source)
XLA Modules:
  0.0 126.1 jit_solution(16012440812342086378)
XLA Ops:
  0.0 0.0 copy-start.8
  0.0 0.1 pad_add_fusion.at_ref
  0.1 0.0 copy-start.1
  0.1 1.5 %copy-done.1 = bf16[16384,56]{0,1:T(8,128)(2,1)S(1)} copy-done((bf16[16384,56]{0,1:T(8,128)(2,1)S(1)}, bf16[16384,56]{0,1:T(8,128)(2,1)}, u32[]{:S(2)}) %copy-start.1) | copy-done | bytes 1835032
  1.6 0.0 copy-start.4
  1.6 0.0 copy-start.5
  1.6 0.0 copy-start.6
  1.6 0.0 copy-start.2
  1.6 0.0 copy-start.3
  1.6 2.1 %blocks_kernel.1 = (bf16[2,2,56,1024]{3,2,1,0:T(8,128)(2,1)S(1)}, bf16[2,2,56,1024]{3,2,1,0:T(8,128)(2,1)}, bf16[2,2,56,1024]{3,2,1,0:T(8,128)(2,1)}, bf16[2,2,56,1024]{3,2,1,0:T(8,128)(2,1)S(1)}) custom-call(s32[2]{0:T(128)S(1)} %pad_add_fusion.at_ref, bf16[56,16384]{1,0:T(8,128)(2,1)S(1)} %bitcast.17), custom_call_target="tpu_custom_call" | custom-call | tf_op jit(solution)/shard_map/weights/blocks_kernel/pallas_call | solution.py:44
  3.7 0.0 copy-done.8
  3.7 0.0 copy-done.4
  3.7 0.0 copy-done.5
  3.7 0.0 copy-done.6
  3.7 1.8 %slices_kernel.1 = bf16[8,144,128]{2,1,0:T(8,128)(2,1)} custom-call(s32[8]{0:T(128)S(1)} %copy-done.8, bf16[8,1536]{1,0:T(8,128)(2,1)S(1)} %copy-done.6, bf16[64,1024]{1,0:T(8,128)(2,1)S(1)} %copy-done.4, bf16[64,1024]{1,0:T(8,128)(2,1)S(1)} %copy-done.5, bf16[2,2,56,1024]{3,2,1,0:T(8,128)(2,1)S(1)} %get-tuple-element.11.early_ref.refs_0_), custom_call_target="tpu_custom_call" | custom-call | tf_op jit(solution)/shard_map/queries/slices_kernel/pallas_call | solution.py:44
  5.5 5.2 %all-to-all-start = ((bf16[8,144,128]{2,1,0:T(8,128)(2,1)}), bf16[8,144,128]{2,1,0:T(8,128)(2,1)S(1)}, u32[]{:S(2)}, u32[]{:S(2)}) async-start(bf16[8,144,128]{2,1,0:T(8,128)(2,1)} %slices_kernel.1), calls=%async_computation | async-start | bytes 589824 | tf_op jit(solution)/shard_map/queries/all_to_all | solution.py:38
  10.7 1.6 %collective-permute-start = (bf16[2,2,56,1024]{3,2,1,0:T(8,128)(2,1)}, bf16[2,2,56,1024]{3,2,1,0:T(8,128)(2,1)S(1)}, u32[]{:S(2)}, u32[]{:S(2)}) collective-permute-start(bf16[2,2,56,1024]{3,2,1,0:T(8,128)(2,1)} %get-tuple-element.12), channel_id=1, source_target_pairs={{0,2},{1,3},{2,0},{3,1},{4,6},{5,7},{6,4},{7,5},{8,10},{9,11},{10,... | collective-permute-start | bytes 1376264 | tf_op jit(solution)/shard_map/weights/ppermute | solution.py:34
  12.4 3.3 %collective-permute-start.1 = (bf16[2,2,56,1024]{3,2,1,0:T(8,128)(2,1)}, bf16[2,2,56,1024]{3,2,1,0:T(8,128)(2,1)S(1)}, u32[]{:S(2)}, u32[]{:S(2)}) collective-permute-start(bf16[2,2,56,1024]{3,2,1,0:T(8,128)(2,1)} %get-tuple-element.13), channel_id=1, source_target_pairs={{0,4},{1,5},{2,6},{3,7},{4,0},{5,1},{6,2},{7,3},{8,12},{9,13},{10,... | collective-permute-start | bytes 1376264 | tf_op jit(solution)/shard_map/weights/ppermute | solution.py:34
  15.7 0.0 collective-permute-start.2
  15.7 0.0 all-to-all-done.got_ref.first_ref
  15.7 0.0 copy-done.2
  15.7 0.0 copy-done.3
  15.7 1.6 %partial_kernel.1 = f32[8,64,192]{2,1,0:T(8,128)} custom-call(bf16[8,144,128]{2,1,0:T(8,128)(2,1)S(1)} %all-to-all-done.got_ref.first_ref, bf16[192,1024]{1,0:T(8,128)(2,1)S(1)} %copy-done.2, bf16[192,512]{1,0:T(8,128)(2,1)S(1)} %copy-done.3), custom_call_target="tpu_custom_call" | custom-call | tf_op jit(solution)/shard_map/queries/partial_kernel/pallas_call | solution.py:44
  17.3 5.2 %all-to-all-start.1 = ((f32[8,64,192]{2,1,0:T(8,128)}), f32[8,64,192]{2,1,0:T(8,128)S(1)}, u32[]{:S(2)}, u32[]{:S(2)}) async-start(f32[8,64,192]{2,1,0:T(8,128)} %partial_kernel.1), calls=%async_computation.1 | async-start | bytes 1048576 | tf_op jit(solution)/shard_map/queries/all_to_all | solution.py:38
  22.4 0.2 add_reduce_fusion
  22.6 0.1 add.19
  22.7 0.2 multiply_sine_fusion
  22.9 0.0 collective-permute-done.refs_0_.refs_1_
  22.9 12.2 %collective-permute-done.1.refs_1_.refs_2_ = bf16[2,2,56,1024]{3,2,1,0:T(8,128)(2,1)S(1)} collective-permute-done((bf16[2,2,56,1024]{3,2,1,0:T(8,128)(2,1)}, bf16[2,2,56,1024]{3,2,1,0:T(8,128)(2,1)S(1)}, u32[]{:S(2)}, u32[]{:S(2)}) %collective-permute-start.1) | collective-permute-done | bytes 458784 | tf_op jit(solution)/shard_map/weights/ppermute | solution.py:34
  35.1 1.9 %collective-permute-done.2.refs_2_.refs_3_ = bf16[2,2,56,1024]{3,2,1,0:T(8,128)(2,1)S(1)} collective-permute-done((bf16[2,2,56,1024]{3,2,1,0:T(8,128)(2,1)S(1)}, bf16[2,2,56,1024]{3,2,1,0:T(8,128)(2,1)S(1)}, u32[]{:S(2)}, u32[]{:S(2)}) %collective-permute-start.2) | collective-permute-done | bytes 458784 | tf_op jit(solution)/shard_map/weights/ppermute | solution.py:34
  36.9 0.0 all-to-all-done.1.part_ref
  36.9 0.0 copy-start.7
  36.9 0.2 query_kernel.1
  37.2 16.8 %all_to_all.30 = bf16[64,8,576]{2,1,0:T(8,128)(2,1)S(1)} all-to-all(bf16[64,8,576]{2,1,0:T(8,128)(2,1)S(1)} %bitcast.16), channel_id=1, replica_groups=mesh['section'=8,'yh'=2,'z'=4,'core'=2] {'section','yh','z'}, dimensions={0} | all-to-all | bytes 1179648 | tf_op jit(solution)/shard_map/queries/all_to_all | solution.py:38
  54.0 3.9 %collective-permute-start.3 = (bf16[64,8,576]{2,1,0:T(8,128)(2,1)S(1)}, bf16[64,8,576]{2,1,0:T(8,128)(2,1)S(1)}, u32[]{:S(2)}, u32[]{:S(2)}) collective-permute-start(bf16[64,8,576]{2,1,0:T(8,128)(2,1)S(1)} %all_to_all.30), channel_id=1, source_target_pairs={{0,1},{1,0},{2,3},{3,2},{4,5},{5,4},{6,7},{7,6},{8,9},{9,8},{10,11... | collective-permute-start | bytes 1769480 | tf_op jit(solution)/shard_map/queries/ppermute | solution.py:34
  58.0 0.1 pad_add_fusion.1.at_ref
  58.0 1.6 %collective-permute-done.3 = bf16[64,8,576]{2,1,0:T(8,128)(2,1)S(1)} collective-permute-done((bf16[64,8,576]{2,1,0:T(8,128)(2,1)S(1)}, bf16[64,8,576]{2,1,0:T(8,128)(2,1)S(1)}, u32[]{:S(2)}, u32[]{:S(2)}) %collective-permute-start.3) | collective-permute-done | bytes 589856 | tf_op jit(solution)/shard_map/queries/ppermute | solution.py:34
  59.7 0.0 copy-done.7
  59.7 0.0 copy-start
  59.7 2.3 %copy-done = bf16[8,512,576]{1,2,0:T(8,128)(2,1)S(1)} copy-done((bf16[8,512,576]{1,2,0:T(8,128)(2,1)S(1)}, bf16[8,512,576]{1,2,0:T(8,128)(2,1)}, u32[]{:S(2)}) %copy-start) | copy-done | bytes 4718616
  62.0 7.0 %attend_kernel.1 = (f32[5,512,128]{2,1,0:T(8,128)S(1)}, bf16[512,640]{1,0:T(8,128)(2,1)S(1)}) custom-call(s32[8]{0:T(128)S(1)} %copy-done.8, s32[2]{0:T(128)S(1)} %pad_add_fusion.1.at_ref, bf16[512,576]{1,0:T(8,128)(2,1)S(1)} %bitcast.13, bf16[512,576]{1,0:T(8,128)(2,1)S(1)} %bitcast.18, bf16[8,576,512]{2,1,0:T(8,128)(2,1)S(1)} %bitcast.12, ...), custom_call_target="tpu_custom_call" | custom-call | tf_op jit(solution)/shard_map/attention/attend_kernel/pallas_call | solution.py:44
  69.0 0.4 collective-permute-start.4
  69.5 1.8 %pick_kernel.1 = bf16[4,2,56,1024]{3,2,1,0:T(8,128)(2,1)S(1)} custom-call(s32[2]{0:T(128)S(1)} %pad_add_fusion.at_ref, bf16[2,2,56,1024]{3,2,1,0:T(8,128)(2,1)S(1)} %get-tuple-element.11.early_ref.refs_0_, bf16[2,2,56,1024]{3,2,1,0:T(8,128)(2,1)S(1)} %collective-permute-done.refs_0_.refs_1_, ...), custom_call_target="tpu_custom_call" | custom-call | tf_op jit(solution)/shard_map/weights/pick_kernel/pallas_call | solution.py:44
  71.3 0.2 collective-permute-start.5
  71.5 0.0 collective-permute-done.4.got_ref
  71.5 0.6 merge_kernel.1
  72.1 18.4 %all_to_all.31 = bf16[64,8,640]{2,1,0:T(8,128)(2,1)S(1)} all-to-all(bf16[64,8,640]{2,1,0:T(8,128)(2,1)S(1)} %bitcast.14), channel_id=1, replica_groups=mesh['section'=8,'yh'=2,'z'=4,'core'=2] {'section','yh','z'}, dimensions={0} | all-to-all | bytes 1310720 | tf_op jit(solution)/shard_map/attention/all_to_all | solution.py:38
  90.5 1.2 combine_kernel.1
  91.7 4.5 %all-to-all-start.4 = ((bf16[16,64,128]{2,1,0:T(8,128)(2,1)}), bf16[16,64,128]{2,1,0:T(8,128)(2,1)S(1)}, u32[]{:S(2)}, u32[]{:S(2)}) async-start(bf16[16,64,128]{2,1,0:T(8,128)(2,1)} %combine_kernel.1), calls=%async_computation.4 | async-start | bytes 524288 | tf_op jit(solution)/shard_map/output/all_to_all | solution.py:38
  96.2 0.0 collective-permute-done.5.refs_4_
  96.2 5.6 %all-to-all-done.4.mid_ref = bf16[16,64,128]{2,1,0:T(8,128)(2,1)S(1)} async-done(((bf16[16,64,128]{2,1,0:T(8,128)(2,1)}), bf16[16,64,128]{2,1,0:T(8,128)(2,1)S(1)}, u32[]{:S(2)}, u32[]{:S(2)}) %all-to-all-start.4) | async-done | bytes 262176 | tf_op jit(solution)/shard_map/output/all_to_all | solution.py:38
  101.8 1.9 %project_kernel.1 = f32[64,512]{1,0:T(8,128)S(1)} custom-call(s32[2]{0:T(128)S(1)} %pad_add_fusion.at_ref, bf16[16,64,128]{2,1,0:T(8,128)(2,1)S(1)} %all-to-all-done.4.mid_ref, bf16[2,2,56,1024]{3,2,1,0:T(8,128)(2,1)S(1)} %get-tuple-element.11.early_ref.refs_0_, bf16[2,2,56,1024]{3,2,1,0:T(8,128)(2,1)S(1)} %collective-permute-done.refs_0_.refs_1_, ...), custom_call_target="tpu_custom_call" | custom-call | tf_op jit(solution)/shard_map/output/project_kernel/pallas_call | solution.py:44
  103.7 11.0 %all_to_all.32.share_ref = f32[8,8,512]{2,1,0:T(8,128)S(1)} all-to-all(f32[8,8,512]{2,1,0:T(8,128)S(1)} %bitcast.19), channel_id=1, replica_groups=mesh['section'=8,'yh'=2,'z'=4,'core'=2] {'z','core'}, dimensions={0} | all-to-all | bytes 262144 | tf_op jit(solution)/shard_map/output/all_to_all | solution.py:38
  114.7 0.1 total_kernel.1
  114.8 5.7 %collective-permute-start.6 = (bf16[8,448]{1,0:T(8,128)(2,1)S(1)}, bf16[8,448]{1,0:T(8,128)(2,1)S(1)}, u32[]{:S(2)}, u32[]{:S(2)}) collective-permute-start(bf16[8,448]{1,0:T(8,128)(2,1)S(1)} %total_kernel.1), channel_id=1, source_target_pairs={{0,0},{1,16},{2,32},{3,48},{4,64},{5,80},{6,96},{7,112},{8,1},{9,1... | collective-permute-start | bytes 21512 | tf_op jit(solution)/shard_map/output/ppermute | solution.py:414
  120.5 5.0 %collective-permute-done.6 = bf16[8,448]{1,0:T(8,128)(2,1)S(1)} collective-permute-done((bf16[8,448]{1,0:T(8,128)(2,1)S(1)}, bf16[8,448]{1,0:T(8,128)(2,1)S(1)}, u32[]{:S(2)}, u32[]{:S(2)}) %collective-permute-start.6) | collective-permute-done | bytes 7200 | tf_op jit(solution)/shard_map/output/ppermute | solution.py:414
  125.5 0.6 copy.11
  (1 shorter events, 0.0 us)
Async XLA Ops:
  0.0 3.7 %copy-start.8 = (s32[8]{0:T(128)S(1)}, s32[8]{0:T(128)}, u32[]{:S(2)}) copy-start(s32[8]{0:T(128)} %len_ref.1) | copy-start | bytes 100
  0.1 1.5 %copy-start.1 = (bf16[16384,56]{0,1:T(8,128)(2,1)S(1)}, bf16[16384,56]{0,1:T(8,128)(2,1)}, u32[]{:S(2)}) copy-start(bf16[16384,56]{0,1:T(8,128)(2,1)} %param.14) | copy-start | bytes 5505028
  1.6 2.1 %copy-start.4 = (bf16[64,1024]{1,0:T(8,128)(2,1)S(1)}, bf16[64,1024]{1,0:T(8,128)(2,1)}, u32[]{:S(2)}) copy-start(bf16[64,1024]{1,0:T(8,128)(2,1)} %key_ref.1) | copy-start | bytes 393220
  1.6 2.1 %copy-start.5 = (bf16[64,1024]{1,0:T(8,128)(2,1)S(1)}, bf16[64,1024]{1,0:T(8,128)(2,1)}, u32[]{:S(2)}) copy-start(bf16[64,1024]{1,0:T(8,128)(2,1)} %value_ref.1) | copy-start | bytes 393220
  1.6 2.1 %copy-start.6 = (bf16[8,1536]{1,0:T(8,128)(2,1)S(1)}, bf16[8,1536]{1,0:T(8,128)(2,1)}, u32[]{:S(2)}) copy-start(bf16[8,1536]{1,0:T(8,128)(2,1)} %query_ref.1) | copy-start | bytes 73732
  1.6 14.1 %copy-start.2 = (bf16[192,1024]{1,0:T(8,128)(2,1)S(1)}, bf16[192,1024]{1,0:T(8,128)(2,1)}, u32[]{:S(2)}) copy-start(bf16[192,1024]{1,0:T(8,128)(2,1)} %up_hbm.1) | copy-start | bytes 1179652
  1.6 14.1 %copy-start.3 = (bf16[192,512]{1,0:T(8,128)(2,1)S(1)}, bf16[192,512]{1,0:T(8,128)(2,1)}, u32[]{:S(2)}) copy-start(bf16[192,512]{1,0:T(8,128)(2,1)} %rope_hbm.1) | copy-start | bytes 589828
  5.5 10.2 %all-to-all-start = ((bf16[8,144,128]{2,1,0:T(8,128)(2,1)}), bf16[8,144,128]{2,1,0:T(8,128)(2,1)S(1)}, u32[]{:S(2)}, u32[]{:S(2)}) async-start(bf16[8,144,128]{2,1,0:T(8,128)(2,1)} %slices_kernel.1), calls=%async_computation | async-start | bytes 589824 | tf_op jit(solution)/shard_map/queries/all_to_all | solution.py:38
  10.7 12.2 %collective-permute-start = (bf16[2,2,56,1024]{3,2,1,0:T(8,128)(2,1)}, bf16[2,2,56,1024]{3,2,1,0:T(8,128)(2,1)S(1)}, u32[]{:S(2)}, u32[]{:S(2)}) collective-permute-start(bf16[2,2,56,1024]{3,2,1,0:T(8,128)(2,1)} %get-tuple-element.12), channel_id=1, source_target_pairs={{0,2},{1,3},{2,0},{3,1},{4,6},{5,7},{6,4},{7,5},{8,10},{9,11},{10,... | collective-permute-start | bytes 1376264 | tf_op jit(solution)/shard_map/weights/ppermute | solution.py:34
  12.4 22.7 %collective-permute-start.1 = (bf16[2,2,56,1024]{3,2,1,0:T(8,128)(2,1)}, bf16[2,2,56,1024]{3,2,1,0:T(8,128)(2,1)S(1)}, u32[]{:S(2)}, u32[]{:S(2)}) collective-permute-start(bf16[2,2,56,1024]{3,2,1,0:T(8,128)(2,1)} %get-tuple-element.13), channel_id=1, source_target_pairs={{0,4},{1,5},{2,6},{3,7},{4,0},{5,1},{6,2},{7,3},{8,12},{9,13},{10,... | collective-permute-start | bytes 1376264 | tf_op jit(solution)/shard_map/weights/ppermute | solution.py:34
  15.7 21.3 %collective-permute-start.2 = (bf16[2,2,56,1024]{3,2,1,0:T(8,128)(2,1)S(1)}, bf16[2,2,56,1024]{3,2,1,0:T(8,128)(2,1)S(1)}, u32[]{:S(2)}, u32[]{:S(2)}) collective-permute-start(bf16[2,2,56,1024]{3,2,1,0:T(8,128)(2,1)S(1)} %get-tuple-element.14), channel_id=1, source_target_pairs={{0,6},{1,7},{2,4},{3,5},{4,2},{5,3},{6,0},{7,1},{8,14},{9,15},{10,... | collective-permute-start | bytes 1376264 | tf_op jit(solution)/shard_map/weights/ppermute | solution.py:34
  17.3 19.7 %all-to-all-start.1 = ((f32[8,64,192]{2,1,0:T(8,128)}), f32[8,64,192]{2,1,0:T(8,128)S(1)}, u32[]{:S(2)}, u32[]{:S(2)}) async-start(f32[8,64,192]{2,1,0:T(8,128)} %partial_kernel.1), calls=%async_computation.1 | async-start | bytes 1048576 | tf_op jit(solution)/shard_map/queries/all_to_all | solution.py:38
  36.9 22.8 %copy-start.7 = (bf16[8,576]{1,0:T(8,128)(2,1)S(1)}, bf16[8,576]{1,0:T(8,128)(2,1)}, u32[]{:S(2)}) copy-start(bf16[8,576]{1,0:T(8,128)(2,1)} %new_ref.1) | copy-start | bytes 27652
  54.0 5.7 %collective-permute-start.3 = (bf16[64,8,576]{2,1,0:T(8,128)(2,1)S(1)}, bf16[64,8,576]{2,1,0:T(8,128)(2,1)S(1)}, u32[]{:S(2)}, u32[]{:S(2)}) collective-permute-start(bf16[64,8,576]{2,1,0:T(8,128)(2,1)S(1)} %all_to_all.30), channel_id=1, source_target_pairs={{0,1},{1,0},{2,3},{3,2},{4,5},{5,4},{6,7},{7,6},{8,9},{9,8},{10,11... | collective-permute-start | bytes 1769480 | tf_op jit(solution)/shard_map/queries/ppermute | solution.py:34
  59.7 2.3 %copy-start = (bf16[8,512,576]{1,2,0:T(8,128)(2,1)S(1)}, bf16[8,512,576]{1,2,0:T(8,128)(2,1)}, u32[]{:S(2)}) copy-start(bf16[8,512,576]{1,2,0:T(8,128)(2,1)} %param.15) | copy-start | bytes 14155780
  69.0 2.4 %collective-permute-start.4 = (bf16[512,640]{1,0:T(8,128)(2,1)S(1)}, bf16[512,640]{1,0:T(8,128)(2,1)S(1)}, u32[]{:S(2)}, u32[]{:S(2)}) collective-permute-start(bf16[512,640]{1,0:T(8,128)(2,1)S(1)} %get-tuple-element.16), channel_id=1, source_target_pairs={{0,1},{1,0},{2,3},{3,2},{4,5},{5,4},{6,7},{7,6},{8,9},{9,8},{10,11... | collective-permute-start | bytes 1966088 | tf_op jit(solution)/shard_map/attention/ppermute | solution.py:34
  71.3 25.0 %collective-permute-start.5 = (bf16[4,2,56,1024]{3,2,1,0:T(8,128)(2,1)S(1)}, bf16[4,2,56,1024]{3,2,1,0:T(8,128)(2,1)}, u32[]{:S(2)}, u32[]{:S(2)}) collective-permute-start(bf16[4,2,56,1024]{3,2,1,0:T(8,128)(2,1)S(1)} %pick_kernel.1), channel_id=1, source_target_pairs={{0,1},{1,0},{2,3},{3,2},{4,5},{5,4},{6,7},{7,6},{8,9},{9,8},{10,11... | collective-permute-start | bytes 2752520 | tf_op jit(solution)/shard_map/weights/ppermute | solution.py:34
  91.7 10.1 %all-to-all-start.4 = ((bf16[16,64,128]{2,1,0:T(8,128)(2,1)}), bf16[16,64,128]{2,1,0:T(8,128)(2,1)S(1)}, u32[]{:S(2)}, u32[]{:S(2)}) async-start(bf16[16,64,128]{2,1,0:T(8,128)(2,1)} %combine_kernel.1), calls=%async_computation.4 | async-start | bytes 524288 | tf_op jit(solution)/shard_map/output/all_to_all | solution.py:38
  114.8 10.7 %collective-permute-start.6 = (bf16[8,448]{1,0:T(8,128)(2,1)S(1)}, bf16[8,448]{1,0:T(8,128)(2,1)S(1)}, u32[]{:S(2)}, u32[]{:S(2)}) collective-permute-start(bf16[8,448]{1,0:T(8,128)(2,1)S(1)} %total_kernel.1), channel_id=1, source_target_pairs={{0,0},{1,16},{2,32},{3,48},{4,64},{5,80},{6,96},{7,112},{8,1},{9,1... | collective-permute-start | bytes 21512 | tf_op jit(solution)/shard_map/output/ppermute | solution.py:414
